TPU v7x, 256 devices: a whole 4x4x8 slice. The times are simulated.
256 devices in a mesh: ctx: 32 (over y_lo, z, core), tp: 8 (over y_hi, x).
Axes of the slice: x: 4, y: 4 (y_hi: 2, y_lo: 2; y = y_hi * 2 + y_lo), z: 8, core: 2. Of those that a mesh axis runs over, the one named last changes fastest.
Arguments:
- queries: bfloat16 [8192, 4096], P('ctx', 'tp'), may hold values from -25 to 25
- keys_values: bfloat16 [8192, 2048], P('ctx', 'tp'), may hold values from -5 to 5
- upstream: bfloat16 [8192, 4096], P('ctx', 'tp'), may hold values from -6 to 6
- out_proj: bfloat16 [4096, 4096], P('ctx', 'tp'), may hold values from -0.09375 to 0.09375
- keep_index: int32 [6144], P('ctx'), may hold values from -1 to 255, as said below
Outputs:
- query_grad: bfloat16 [8192, 4096], P('ctx', 'tp')
- kv_grad: bfloat16 [8192, 2048], P('ctx', 'tp')
- out_proj_grad: bfloat16 [4096, 4096], P('ctx', 'tp')
Inputs may be any that keep to these rules, and one draw needn't show every extreme that they name: `keep_index`: each shard's 192 entries list distinct local positions of its kept tokens in ascending order, then -1 in the unused slots; a shard keeps 192 // 3 to 192 tokens, and some shard keeps exactly 192.
All inputs are finite; a program needn't handle non-finite values.
Results may differ from a plain program's by a relative error of at most 0.04.
Values may be sent and summed in bfloat16 or wider, within the bound.
A program may use at most 64 MiB of HBM per device.

v0:
```python
import math

import jax
import jax.numpy as jnp
from jax import lax
from jax.sharding import PartitionSpec as P

HEAD_SIZE = 128


def compact(picker, matrix):
    return jnp.dot(picker, matrix, preferred_element_type=jnp.float32).astype(jnp.bfloat16)


def to_rows(matrix, pair_count, query_group_width):
    slot_count = matrix.shape[0]
    shaped = matrix.reshape(slot_count, pair_count, query_group_width, HEAD_SIZE).transpose(
        1, 0, 2, 3
    )
    return shaped.reshape(pair_count, slot_count * query_group_width, HEAD_SIZE)


def from_rows(stacked, slot_count, query_group_width):
    pair_count = stacked.shape[0]
    shaped = stacked.reshape(pair_count, slot_count, query_group_width, HEAD_SIZE).transpose(
        1, 0, 2, 3
    )
    return shaped.reshape(slot_count, pair_count * query_group_width * HEAD_SIZE)


def split_pairs(kv_block, pair_count):
    block_rows = kv_block.shape[0]
    shaped = kv_block.reshape(block_rows, pair_count, 2, HEAD_SIZE)
    return (shaped[:, :, 0].transpose(1, 0, 2), shaped[:, :, 1].transpose(1, 0, 2))


def over_blocks(step, carry, kv_piece, pos_piece, block_width):
    piece_rows = kv_piece.shape[0]

    def one_block(step_index, current):
        first_row = step_index * block_width
        kv_block = lax.dynamic_slice_in_dim(kv_piece, first_row, block_width, 0)
        pos_block = lax.dynamic_slice_in_dim(pos_piece, first_row, block_width, 0)
        return step(current, kv_block, pos_block, first_row)

    return lax.fori_loop(0, piece_rows // block_width, one_block, carry)


def keep_state(current):
    return current


def shards(queries, keys_values, upstream, out_proj, keep_index):
    local_rows = queries.shape[0]
    slot_count = keep_index.shape[0]
    head_cols = out_proj.shape[1]
    pair_count = keys_values.shape[1] // (2 * HEAD_SIZE)
    query_group_width = head_cols // HEAD_SIZE // pair_count
    score_scale = 1.0 / math.sqrt(HEAD_SIZE)
    shard_count = lax.axis_size("ctx")
    block_width = 4 * slot_count
    picker = (keep_index[:, None] == jnp.arange(local_rows, dtype=jnp.int32)[None, :]).astype(
        jnp.bfloat16
    )
    offset = lax.axis_index("ctx") * local_rows
    filled = keep_index >= 0
    query_pos = jnp.where(filled, keep_index + offset, -1)
    key_pos = jnp.where(filled, keep_index + offset, 1 << 30)
    query_kept = compact(picker, queries)
    kv_kept = compact(picker, keys_values)
    upstream_kept = compact(picker, upstream)
    upstream_full = lax.all_gather(upstream_kept, "tp", axis=1, tiled=True)
    column_list = upstream_full
    grad_heads = jnp.dot(
        column_list,
        lax.all_gather(out_proj, "ctx", axis=0, tiled=True),
        preferred_element_type=jnp.float32,
    ).astype(jnp.bfloat16)
    query_row_set = to_rows(query_kept, pair_count, query_group_width)
    gradient_rows = to_rows(grad_heads, pair_count, query_group_width)
    row_pos = jnp.repeat(query_pos, query_group_width)
    newest = jnp.max(query_pos)
    row_total = slot_count * query_group_width

    def masked_scores(key_tile_block, pos_block):
        scores = (
            jnp.einsum(
                "mfy,mwy->mfw", query_row_set, key_tile_block, preferred_element_type=jnp.float32
            )
            * score_scale
        )
        allowed = pos_block[None, :] <= row_pos[:, None]
        return jnp.where(allowed[None], scores, jnp.float32(-1e30))

    def forward_step(carry, kv_block, pos_block, start_row):

        def forward_compute(current):
            running_max, running_sum, weighted = current
            key_tile_block, value_tile_block = split_pairs(kv_block, pair_count)
            scores = masked_scores(key_tile_block, pos_block)
            new_max = jnp.maximum(running_max, jnp.max(scores, axis=2))
            shrink = jnp.exp(running_max - new_max)
            weights = jnp.exp(scores - new_max[:, :, None])
            running_sum = running_sum * shrink + jnp.sum(weights, axis=2)
            weighted = weighted * shrink[:, :, None] + jnp.einsum(
                "inc,icm->inm",
                weights,
                value_tile_block.astype(jnp.float32),
                precision=lax.Precision.HIGHEST,
                preferred_element_type=jnp.float32,
            )
            return (new_max, running_sum, weighted)

        return lax.cond(jnp.min(pos_block) <= newest, forward_compute, keep_state, carry)

    forward_init = (
        jnp.full((pair_count, row_total), -1e30, jnp.float32),
        jnp.zeros((pair_count, row_total), jnp.float32),
        jnp.zeros((pair_count, row_total, HEAD_SIZE), jnp.float32),
    )
    shard_piece = (
        lax.all_gather(kv_kept, "ctx", axis=0, tiled=True),
        lax.all_gather(key_pos, "ctx", axis=0, tiled=True),
    )
    running_max, running_sum, weighted = over_blocks(
        forward_step, forward_init, shard_piece[0], shard_piece[1], block_width
    )
    attn_rows = (weighted / running_sum[:, :, None]).astype(jnp.bfloat16)
    log_total = running_max + jnp.log(running_sum)
    delta = jnp.sum(gradient_rows.astype(jnp.float32) * attn_rows.astype(jnp.float32), axis=2)
    attn_kept = from_rows(attn_rows, slot_count, query_group_width)

    def backward_step(carry, kv_block, pos_block, start_row):

        def backward_compute(current):
            query_grad, key_grads = current
            key_tile_block, value_tile_block = split_pairs(kv_block, pair_count)
            scores = masked_scores(key_tile_block, pos_block)
            probs_full = jnp.exp(scores - log_total[:, :, None])
            probability_half = probs_full.astype(jnp.bfloat16)
            pushes = jnp.einsum(
                "mfy,mwy->mfw", gradient_rows, value_tile_block, preferred_element_type=jnp.float32
            )
            alibi_slopes = (probs_full * (pushes - delta[:, :, None]) * score_scale).astype(
                jnp.bfloat16
            )
            query_grad = query_grad + jnp.einsum(
                "inc,icm->inm", alibi_slopes, key_tile_block, preferred_element_type=jnp.float32
            )
            key_portion = jnp.einsum(
                "hgn,hgl->hnl", alibi_slopes, query_row_set, preferred_element_type=jnp.float32
            )
            value_portion = jnp.einsum(
                "hgn,hgl->hnl", probability_half, gradient_rows, preferred_element_type=jnp.float32
            )
            key_update = jnp.stack([key_portion, value_portion], axis=2).transpose(1, 0, 2, 3)
            key_update = key_update.reshape(kv_block.shape[0], pair_count * 2 * HEAD_SIZE)
            key_grads = lax.dynamic_update_slice_in_dim(key_grads, key_update, start_row, 0)
            return (query_grad, key_grads)

        return lax.cond(jnp.min(pos_block) <= newest, backward_compute, keep_state, carry)

    backward_init = (
        jnp.zeros((pair_count, row_total, HEAD_SIZE), jnp.float32),
        jnp.zeros((slot_count * shard_count, pair_count * 2 * HEAD_SIZE), jnp.float32),
    )
    shard_piece = (
        lax.all_gather(kv_kept, "ctx", axis=0, tiled=True),
        lax.all_gather(key_pos, "ctx", axis=0, tiled=True),
    )
    query_grad, key_grads = over_blocks(
        backward_step, backward_init, shard_piece[0], shard_piece[1], block_width
    )
    query_slots = from_rows(query_grad.astype(jnp.bfloat16), slot_count, query_group_width)
    query_out = jnp.dot(picker.T, query_slots, preferred_element_type=jnp.float32).astype(
        jnp.bfloat16
    )
    summed_keys = lax.psum_scatter(key_grads, "ctx", scatter_dimension=0, tiled=True).astype(
        jnp.bfloat16
    )
    key_value_output = jnp.dot(picker.T, summed_keys, preferred_element_type=jnp.float32).astype(
        jnp.bfloat16
    )
    column_list = upstream_full
    proj_grad = lax.psum_scatter(
        jnp.dot(column_list.T, attn_kept, preferred_element_type=jnp.float32),
        "ctx",
        scatter_dimension=0,
        tiled=True,
    )
    return (query_out, key_value_output, proj_grad.astype(jnp.bfloat16))


def solution(mesh):
    in_specs = (P("ctx", "tp"), P("ctx", "tp"), P("ctx", "tp"), P("ctx", "tp"), P("ctx"))
    out_specs = (P("ctx", "tp"), P("ctx", "tp"), P("ctx", "tp"))
    return jax.shard_map(shards, mesh=mesh, in_specs=in_specs, out_specs=out_specs, check_vma=False)
```

profile of v0, /device:TPU:1, one launch (start us, length us, event | category | flops | bytes accessed | tf_op | source)
XLA Modules:
  0.0 535.7 jit_solution(7665312065892714147)
XLA Ops:
  7.2 1.8 convolution_convert_fusion.5
  9.1 1.6 convolution_convert_fusion.2
  10.8 0.7 all-gather.8.cloned.1.call-update
  11.6 1.2 convolution_convert_fusion.3
  12.9 1.3 dynamic-slice
  14.9 1.4 fusion.31
  16.3 108.4 %all-reduce = s32[6144]{0:T(1024)S(1)} all-reduce(s32[6144]{0:T(1024)S(1)} %get-tuple-element.621), channel_id=1, replica_groups=mesh['ctx'=32,'tp'=8] {'ctx'}, use_global_device_ids=true, to_apply=%add | all-reduce | flops 6144 | bytes 49152
  124.7 4.7 copy.23
  129.5 20.8 %while.34 = (s32[]{:T(128)}, f32[1,768]{1,0:T(1,128)S(1)}, f32[1,768]{1,0:T(1,128)S(1)}, f32[1,768,128]{2,1,0:T(8,128)S(1)}, s32[6144]{0:T(1024)S(1)}, /*index=5...) while((s32[]{:T(128)}, f32[1,768]{1,0:T(1,128)S(1)}, ...), condition=%wide.region_7.8_spmd.clone, body=%wide.region_1.7_spmd.clone.sunk | while | flops 1061293056 | bytes 9319485 | solution.py:46
  129.5 0.8 fusion.48
  131.5 4.4 conditional.6
  131.7 1.0 constant_dynamic-slice_fusion
  132.7 0.6 fusion.32
  133.4 2.1 fusion.7
  136.0 0.8 fusion.48
  138.0 0.8 fusion.48
  140.1 0.8 fusion.48
  142.1 0.8 fusion.48
  144.2 0.8 fusion.48
  146.2 0.8 fusion.48
  148.3 0.8 fusion.48
  150.4 58.5 %all-gather.8.cloned.1.call-done = bf16[4096,512]{1,0:T(8,128)(2,1)} async-done(((bf16[128,512]{1,0:T(8,128)(2,1)}), bf16[4096,512]{1,0:T(8,128)(2,1)}) %all-gather.8.cloned.1.call-update) | async-done | bytes 4194320 | tf_op jit(solution)/shard_map/all_gather | solution.py:76
  208.9 3.6 convolution_convert_fusion.1
  213.0 3.4 broadcast_in_dim.37
  216.4 22.0 %while.35 = (s32[]{:T(128)}, f32[1,768,128]{2,1,0:T(8,128)S(1)}, f32[6144,256]{0,1:T(8,128)}, s32[6144]{0:T(1024)S(1)}, s32[]{:T(128)}, /*index=5*/bf16[6144,256...) while((s32[]{:T(128)}, f32[1,768,128]{2,1,0:T(8,128)S(1)}, ...), condition=%wide.region_13.14_spmd.clone, body=%wide.region_9.13_spmd.clone.sunk | while | flops 760578816 | bytes 17543300 | solution.py:46
  216.4 0.8 fusion.49
  218.5 5.3 conditional.7
  218.7 1.0 constant_dynamic-slice_fusion.1
  219.8 0.8 fusion.14
  220.6 0.6 convolution_bitcast_fusion
  222.2 0.5 convolution_bitcast_fusion.1
  222.8 1.0 constant_dynamic-update-slice_fusion
  223.8 0.8 fusion.49
  225.9 0.8 fusion.49
  228.0 0.8 fusion.49
  230.1 0.8 fusion.49
  232.2 0.8 fusion.49
  234.3 0.8 fusion.49
  236.4 0.8 fusion.49
  238.5 6.7 %copy.24 = f32[6144,256]{1,0:T(8,128)} copy(f32[6144,256]{0,1:T(8,128)} %get-tuple-element.472) | data formatting | bytes 12582912
  245.3 1.2 copy-done.1
  246.5 4.5 fusion.34
  251.7 1.1 convolution_convert_fusion
  252.8 147.8 %reduce-scatter.7.cloned.1.call-done = f32[192,256]{1,0:T(8,128)} async-done(((f32[6144,256]{1,0:T(8,128)}), f32[192,256]{1,0:T(8,128)}) %reduce-scatter.7.cloned.1.call-update) | async-done | bytes 196624
  400.6 1.0 copy.25
  401.6 1.0 convolution_convert_fusion.4
  402.6 125.0 %reduce-scatter.5.cloned.1.call-done = f32[128,512]{1,0:T(8,128)} async-done(((f32[4096,512]{1,0:T(8,128)}), f32[128,512]{1,0:T(8,128)}) %reduce-scatter.5.cloned.1.call-update) | async-done | bytes 262160 | tf_op jit(solution)/shard_map/reduce_scatter | solution.py:185
  527.6 1.6 convert_element_type.81
  (56 shorter events, 3.8 us)
Async XLA Ops:
  7.2 2.0 copy-start
  7.2 117.6 %all-gather.4.cloned.1.call-start = ((), (), s32[]{:S(2)}) async-start(), calls=%async_computation.2 | async-start | bytes 3244032 | tf_op jit(solution)/shard_map/all_gather | solution.py:168
  9.1 141.3 %all-gather.6.cloned.1.call-start = ((), (), s32[]{:S(2)}) async-start(), calls=%async_computation.3 | async-start | bytes 1769472 | tf_op jit(solution)/shard_map/all_gather | solution.py:72
  10.8 198.1 %all-gather.8.cloned.1.call-start = ((), (), s32[]{:S(2)}) async-start(), calls=%async_computation.4 | async-start | bytes 4325376 | tf_op jit(solution)/shard_map/all_gather | solution.py:76
  11.5 389.1 %reduce-scatter.7.cloned.1.call-start = ((), (), s32[]{:S(2)}) async-start(), calls=%async_computation.6 | async-start | bytes 6488064
  245.1 1.4 copy-start.1
  245.1 282.4 %reduce-scatter.5.cloned.1.call-start = ((), (), s32[]{:S(2)}) async-start(), calls=%async_computation.5 | async-start | bytes 8650752 | tf_op jit(solution)/shard_map/reduce_scatter | solution.py:185
  251.0 0.7 copy-start.2
Sparse Core Ops, SparseCore 0:
  10.4 70.1 all-gather.3
  83.7 55.9 all-gather.5
  141.6 67.2 all-gather.7
  245.3 155.2 reduce-scatter.6
  403.0 124.5 reduce-scatter.4
where the time goes:
time: 541 us; the launch traced here: 536 us
  waiting for transfers between devices  332 us (61%)
  blocking collectives  108 us (20%)
  local copies, waits for them, and re-layouts  22.8 us (4%)
  loops' own time  20.9 us (4%)
  matrix products  20.5 us (4%)
  other arithmetic  16.2 us (3%)
  between operations  14.6 us (3%)
    unnamed x6, waiting for transfers between devices  149 us
    reduce_scatter x1, waiting for transfers between devices, shards(): lax.psum_scatter(jnp.dot(column_list.T, attn_kept, preferred_element_type...  125 us
    unnamed x1, blocking collectives  108 us
    all_gather x1, waiting for transfers between devices, shards(): lax.all_gather(out_proj, 'ctx', axis=0, tiled=True)  58.5 us
    another operation x2, loops' own time, over_blocks(): return lax.fori_loop(0, piece_rows // block_width, one_block, carry)  20.6 us
    unnamed x11, local copies, waits for them, and re-layouts  15.4 us
  transfers between devices with their start and end apart: 5, of which 3 were waited for; matrix products, arithmetic and copies ran while one was open for 5% of the time, Pallas kernels for 0%

commit v1 on v0

v1 whole, which is shorter than its diff:
```python
import functools
import math

import jax
import jax.numpy as jnp
from jax import lax
from jax.experimental import pallas as pl
from jax.experimental.pallas import tpu as pltpu
from jax.sharding import PartitionSpec as P

MESH = pl.DeviceIdType.MESH
BF = jnp.bfloat16
F32 = jnp.float32
NEG = -1e30
HEAD = 128
HEADS = 4
SLOTS = 192
ROWS = SLOTS + 16
PAIR = 2 * SLOTS
QROWS = HEADS * SLOTS
TOKENS = 256
NZ = 8
NX = 4
CHUNK = 256
SCALE = 1.0 / math.sqrt(HEAD)
LOG2 = SCALE * math.log2(math.e)
NT = (((1,), (1,)), ((), ()))


def mm(a, b):
    return jnp.dot(a, b, preferred_element_type=F32)


def kernel(
    keep_ref, q_ref, kv_ref, up_ref, w_ref,
    qo_ref, kvo_ref, po_ref,
    kvb, wb, ub, eb, mb, qr, dor, ot, dqt, stat, pickt, attn, doacc,
    pj, pjs, pjy, pjr, dkv, sib, rrx, yrx,
    kv_rs, kv_ss, kvsib_rs, kvsib_ss, kvy_ss,
    w_rs, w_ss, wsib_rs, wsib_ss, wy_rs, wy_ss, wys_rs, wys_ss,
    u_rs, u_ss,
    pjs_rs, pjs_ss, pjy_rs, pjy_ss, pjr_rs, pjr_ss,
    sib_rs, sib_ss, rrx_rs, rrx_ss, yrx_s,
):
    ctx = lax.axis_index("ctx")
    tp = lax.axis_index("tp")
    y = ctx // (2 * NZ)
    z = (ctx // 2) % NZ
    k = ctx % 2
    yh = tp // NX
    x = tp % NX

    def at_z(zz):
        return y * 2 * NZ + (zz % NZ) * 2 + k

    ring = ((at_z(z + 1), tp), (at_z(z + NZ - 1), tp))
    sibling = (ctx + 1 - 2 * k, tp)
    across = ((1 - y) * 2 * NZ + z * 2 + k, tp)
    xring = ((ctx, yh * NX + (x + 1) % NX), (ctx, yh * NX + (x + NX - 1) % NX))
    yh_peer = (ctx, (1 - yh) * NX + x)
    upper = y == 1
    lower = y == 0

    barrier = pltpu.get_barrier_semaphore()
    peers = ring + (sibling, across) + xring + (yh_peer,)
    for peer in peers:
        pl.semaphore_signal(barrier, inc=1, device_id=peer, device_id_type=MESH)

    pending = []

    def copy(src, dst, ssem, rsem, dev):
        return pltpu.make_async_remote_copy(
            src_ref=src, dst_ref=dst, send_sem=ssem, recv_sem=rsem,
            device_id=dev, device_id_type=MESH,
        )

    def send(cond, make):
        pending.append((cond, make))
        make().start()

    def got(ref, sem):
        copy(ref, ref, sem, sem, sibling).wait_recv()

    keep = keep_ref[...]
    pick_t = jnp.where(
        lax.broadcasted_iota(jnp.int32, (TOKENS, TOKENS), 0) == keep, 1.0, 0.0
    ).astype(F32)
    pickt[...] = pick_t.astype(BF)
    pick = pick_t.T.astype(BF)[:SLOTS]
    count = jnp.sum(jnp.where(keep >= 0, 1.0, 0.0), axis=1, keepdims=True)
    kvb[ctx, 0:SLOTS, :] = mm(pick, kv_ref[...]).astype(BF)
    kvb[ctx, SLOTS:ROWS, :] = jnp.broadcast_to(count, (ROWS - SLOTS, 2 * HEAD)).astype(BF)
    wb[ctx] = w_ref[...]
    ub[tp] = mm(pick, up_ref[...]).astype(BF)
    q_kept = mm(pick, q_ref[...]).astype(BF)
    for h in range(HEADS):
        qr[h * SLOTS:(h + 1) * SLOTS, :] = q_kept[:, h * HEAD:(h + 1) * HEAD]

    pl.semaphore_wait(barrier, len(peers))

    def slot_of(row, side, dist):
        zz = (z + NZ - dist) % NZ if side == 0 else (z + dist) % NZ
        return row * 2 * NZ + zz * 2 + k

    def kv_part(slot, side, dist):
        if dist < 4:
            return kvb.at[slot]
        return kvb.at[slot, pl.ds(0, 112)] if side == 0 else kvb.at[slot, pl.ds(112, 96)]

    def w_part(slot, side, dist):
        if dist < 4:
            return wb.at[slot]
        return wb.at[slot, pl.ds(side * 64, 64)]

    rows_of = (y, 0)

    def kv_ring(q, side, dist, cond=None):
        part = lambda: kv_part(slot_of(rows_of[q], side, dist), side, dist + 1)
        send(cond, lambda: copy(
            part(), part(), kv_ss.at[q, side, dist], kv_rs.at[q, side, dist + 1], ring[side]))

    def kv_sib(q, side, dist, cond=None):
        part = lambda: kv_part(slot_of(rows_of[q], side, dist), side, dist)
        send(cond, lambda: copy(
            part(), part(), kvsib_ss.at[q, side, dist], kvsib_rs.at[q, side, dist], sibling))

    def kv_sib_got(q, side, dist):
        slot = slot_of(rows_of[q], side, dist) + 1 - 2 * k
        got(kv_part(slot, side, dist), kvsib_rs.at[q, side, dist])

    def w_ring(side, dist):
        part = lambda: w_part(slot_of(y, side, dist), side, dist + 1)
        send(None, lambda: copy(
            part(), part(), w_ss.at[side, dist], w_rs.at[side, dist + 1], ring[side]))

    def w_out(side, dist):
        part = lambda: w_part(slot_of(y, side, dist), side, dist)
        send(None, lambda: copy(
            part(), part(), wy_ss.at[side, dist], wy_rs.at[side, dist], across))
        send(None, lambda: copy(
            part(), part(), wsib_ss.at[side, dist], wsib_rs.at[side, dist], sibling))

    def w_across(side, dist):
        part = lambda: w_part(slot_of(1 - y, side, dist), side, dist)
        got(part(), wy_rs.at[side, dist])
        send(None, lambda: copy(
            part(), part(), wys_ss.at[side, dist], wys_rs.at[side, dist], sibling))

    def w_sib_got(side, dist):
        turn = 1 - 2 * k
        got(w_part(slot_of(y, side, dist) + turn, side, dist), wsib_rs.at[side, dist])
        got(w_part(slot_of(1 - y, side, dist) + turn, side, dist), wys_rs.at[side, dist])

    def u_slot(h, side, dist):
        xx = (x + NX - dist) % NX if side == 0 else (x + dist) % NX
        return (yh if h == 0 else 1 - yh) * NX + xx

    def u_part(h, side, dist, half):
        slot = u_slot(h, side, dist)
        return ub.at[slot, pl.ds(side * 96, 96)] if half else ub.at[slot]

    def u_ring(h, side, dist):
        part = lambda: u_part(h, side, dist, dist + 1 == 2)
        send(None, lambda: copy(
            part(), part(), u_ss.at[h, side, dist], u_rs.at[h, side, dist + 1], xring[side]))

    def u_got(h, side, dist):
        got(u_part(h, side, dist, dist == 2), u_rs.at[h, side, dist])

    for side in (0, 1):
        kv_ring(0, side, 0)

    @pl.when(lower)
    def _():
        send(lower, lambda: copy(
            kvb.at[ctx], kvb.at[ctx], kvy_ss.at[0], kv_rs.at[1, 0, 0], across))

    kv_sib(0, 0, 0)
    for side in (0, 1):
        w_ring(side, 0)
    w_out(0, 0)
    for side in (0, 1):
        u_ring(0, side, 0)
    send(None, lambda: copy(ub.at[tp], ub.at[tp], u_ss.at[0, 0, 2], u_rs.at[1, 0, 0], yh_peer))

    ot[...] = jnp.zeros_like(ot)
    dqt[...] = jnp.zeros_like(dqt)
    stat[0:1, :] = jnp.full((1, QROWS), NEG, F32)
    stat[1:2, :] = jnp.zeros((1, QROWS), F32)

    def load_pair(p):
        block = kvb[pl.ds(2 * p, 2), 0:SLOTS, :]
        return (block[:, :, 0:HEAD].reshape(PAIR, HEAD), block[:, :, HEAD:].reshape(PAIR, HEAD))

    def turned(block):
        return block.astype(F32).T.astype(BF)

    def forward_block(p, own):
        keys, values = load_pair(p)
        values_t = turned(values)
        counts = kvb[pl.ds(2 * p, 2), SLOTS:ROWS, 0:HEAD].astype(F32)
        place = lax.broadcasted_iota(jnp.int32, (SLOTS, HEAD), 0).astype(F32)
        bias = jnp.concatenate(
            [jnp.where(place < counts[i, 0:1, :], 0.0, NEG) for i in (0, 1)], axis=0)
        bias = jnp.concatenate([bias] * (CHUNK // HEAD), axis=1)
        for first in range(0, QROWS, CHUNK):
            cols = slice(first, first + CHUNK)
            scores = lax.dot_general(keys, qr[cols, :], NT, preferred_element_type=F32) + bias
            if own:
                row = lax.broadcasted_iota(jnp.int32, (SLOTS, CHUNK), 0)
                col = (lax.broadcasted_iota(jnp.int32, (SLOTS, CHUNK), 1) + first) % SLOTS
                late = jnp.concatenate(
                    [jnp.where(row - col <= (k - i) * 1024, 0.0, NEG) for i in (0, 1)], axis=0)
                scores = scores + late
            old = stat[0:1, cols]
            new = jnp.maximum(old, jnp.max(scores, axis=0, keepdims=True) * LOG2)
            weights = jnp.exp2(scores * LOG2 - new)
            shrink = jnp.exp2(old - new)
            stat[0:1, cols] = new
            stat[1:2, cols] = stat[1:2, cols] * shrink + jnp.sum(weights, axis=0, keepdims=True)
            half = weights.astype(BF)
            eb[p, :, cols] = half
            mb[p, 0:1, cols] = new
            ot[:, cols] = ot[:, cols] * shrink + mm(values_t, half)

    kv_sib_got(0, 0, 0)
    forward_block(y * NZ + z, True)

    @pl.when(upper)
    def _():
        got(kvb.at[slot_of(0, 0, 0)], kv_rs.at[1, 0, 0])
        for side in (0, 1):
            kv_ring(1, side, 0, upper)
        kv_sib(1, 0, 0, upper)

    def forward_at(dist):
        sides = (0, 1) if 0 < dist < 4 else (0,)
        halves = (0, 1) if dist > 0 else (0,)
        if dist > 0:
            for side in halves:
                kv_sib_got(0, side, dist)

        @pl.when(upper)
        def _():
            for side in halves:
                kv_sib_got(1, side, dist)

        def step(i, carry):
            q = i // len(sides)
            side = i % len(sides)
            shift = jnp.where(side == 0, NZ - dist, dist)
            zz = (z + shift) % NZ
            needed = jnp.logical_or(
                jnp.logical_and(q == 0, zz < z), jnp.logical_and(q == 1, upper))

            @pl.when(needed)
            def _():
                forward_block(jnp.where(q == 0, y * NZ, 0) + zz, False)

            return carry

        lax.fori_loop(0, 2 * len(sides), step, 0)

    for dist in range(1, 5):
        for side in (0, 1):
            got(kv_part(slot_of(y, side, dist), side, dist), kv_rs.at[0, side, dist])
            if dist < 4:
                kv_ring(0, side, dist)
            kv_sib(0, side, dist)
        for side in (0, 1):
            got(w_part(slot_of(y, side, dist), side, dist), w_rs.at[side, dist])
            if dist < 4:
                w_ring(side, dist)
            w_out(side, dist)

        @pl.when(upper)
        def _():
            for side in (0, 1):
                got(kv_part(slot_of(0, side, dist), side, dist), kv_rs.at[1, side, dist])
                if dist < 4:
                    kv_ring(1, side, dist, upper)
                kv_sib(1, side, dist, upper)

        if dist == 1:
            for side in (0, 1):
                u_got(0, side, 1)
                u_ring(0, side, 1)
            got(ub.at[u_slot(1, 0, 0)], u_rs.at[1, 0, 0])
            for side in (0, 1):
                u_ring(1, side, 0)
        if dist == 2:
            for side in (0, 1):
                u_got(1, side, 1)
                u_ring(1, side, 1)
        forward_at(dist - 1)
        for side in ((0, 1) if dist > 1 else (0,)):
            w_across(side, dist - 1)
    forward_at(4)

    total = stat[1:2, :]
    inv = 1.0 / total
    stat[1:2, :] = inv
    attn_t = (ot[...] * inv).astype(BF).astype(F32)
    ot[...] = attn_t
    attn_rows = attn_t.T.astype(BF)
    for h in range(HEADS):
        attn[0:SLOTS, h * HEAD:(h + 1) * HEAD] = attn_rows[h * SLOTS:(h + 1) * SLOTS, :]
    attn[SLOTS:, :] = jnp.zeros((TOKENS - SLOTS, HEADS * HEAD), BF)

    for h in (0, 1):
        for side in (0, 1):
            u_got(h, side, 2)

    def proj_terms(i, carry):
        block = jnp.concatenate(
            [ub[i].astype(F32), jnp.zeros((TOKENS - SLOTS, HEADS * HEAD), F32)], axis=0)
        term = mm(block.T.astype(BF), attn[...]).astype(BF)
        pj[pl.ds(4 * i, 4)] = term.reshape(4, 128, HEADS * HEAD)
        return carry

    lax.fori_loop(0, 8, proj_terms, 0)

    def pj_slot(row, j, core):
        return row * 2 * NZ + ((z + j) % NZ) * 2 + core

    order = (4, 3, 5, 2, 6, 1, 7, 0)
    for turn in (1, 0):
        row = y if turn == 0 else 1 - y
        for j in order:
            def make(row=row, j=j, turn=turn):
                return copy(pj.at[pj_slot(row, j, 1 - k)], pjs.at[turn, j],
                            pjs_ss.at[turn, j], pjs_rs.at[turn, j], sibling)
            send(None, make)

    for side in (0, 1):
        w_across(side, 4)
    for dist in range(0, 5):
        for side in ((0, 1) if dist > 0 else (0,)):
            w_sib_got(side, dist)

    doacc[...] = jnp.zeros_like(doacc)

    def head_grads(i, carry):
        doacc[...] += mm(ub[i], wb[pl.ds(4 * i, 4)].reshape(4 * 128, HEADS * HEAD))
        return carry

    lax.fori_loop(0, 8, head_grads, 0)
    for h in range(HEADS):
        grads = doacc[:, h * HEAD:(h + 1) * HEAD].astype(BF)
        dor[h * SLOTS:(h + 1) * SLOTS, :] = grads
    stat[2:3, :] = jnp.sum(dor[...].astype(F32).T * ot[...], axis=0, keepdims=True)

    for j in order:
        got(pjs.at[1, j], pjs_rs.at[1, j])
        slot = pj_slot(1 - y, j, k)
        pj[slot] = (pj[slot].astype(F32) + pjs[1, j].astype(F32)).astype(BF)

        def make(j=j):
            return copy(pj.at[pj_slot(1 - y, j, k)], pjy.at[j],
                        pjy_ss.at[j], pjy_rs.at[j], across)
        send(None, make)

    def backward_block(p, q, j):
        keys, values = load_pair(p)
        keys_t = turned(keys)
        key_grad = jnp.zeros((PAIR, HEAD), F32)
        value_grad = jnp.zeros((PAIR, HEAD), F32)
        for first in range(0, QROWS, CHUNK):
            cols = slice(first, first + CHUNK)
            level = jnp.exp2(mb[p, 0:1, cols] - stat[0:1, cols]) * stat[1:2, cols]
            probs = eb[p, :, cols].astype(F32) * level
            grads = dor[cols, :]
            value_grad = value_grad + mm(probs.astype(BF), grads)
            pushes = lax.dot_general(values, grads, NT, preferred_element_type=F32)
            slopes = (probs * (pushes - stat[2:3, cols])).astype(BF)
            key_grad = key_grad + mm(slopes, qr[cols, :])
            dqt[:, cols] += mm(keys_t, slopes)
        dkv[q, j, :, :, 0:HEAD] = (key_grad * SCALE).astype(BF).reshape(2, SLOTS, HEAD)
        dkv[q, j, :, :, HEAD:] = value_grad.astype(BF).reshape(2, SLOTS, HEAD)

    def sides_of(dist):
        return (0, 1) if 0 < dist < 4 else (0,)

    def j_of(side, dist):
        return dist if side == 0 else NZ - dist

    def backward_at(dist):
        sides = sides_of(dist)

        def step(i, carry):
            q = i // len(sides)
            side = i % len(sides)
            j = jnp.where(side == 0, dist, NZ - dist)
            zz = (z + j) % NZ
            needed = jnp.logical_or(
                jnp.logical_and(q == 0, zz <= z), jnp.logical_and(q == 1, upper))

            @pl.when(needed)
            def _():
                backward_block(jnp.where(q == 0, y * NZ, 0) + zz, q, j)

            @pl.when(jnp.logical_not(needed))
            def _():
                dkv[q, j] = jnp.zeros((2, SLOTS, 2 * HEAD), BF)

            return carry

        lax.fori_loop(0, 2 * len(sides), step, 0)

        def swap(q, cond):
            for side in sides:
                j = j_of(side, dist)
                send(cond, lambda j=j: copy(
                    dkv.at[q, j, 1 - k], sib.at[q, j], sib_ss.at[q, j], sib_rs.at[q, j], sibling))

        swap(0, None)

        @pl.when(upper)
        def _():
            swap(1, upper)

    def add_into(ref, parts):
        value = ref[...].astype(F32)
        for part in parts:
            value = value + part[...].astype(F32)
        ref[...] = value.astype(BF)

    def kv_pass(dist, q, cond):
        for side in sides_of(dist):
            j = j_of(side, dist)
            got(sib.at[q, j], sib_rs.at[q, j])
            add_into(dkv.at[q, j, k], [sib.at[q, j]])
            if dist == 3:
                half = pl.ds(side * 96, 96)
                got(rrx.at[q, side, 3, half], rrx_rs.at[q, side, 3])
                add_into(dkv.at[q, j, k, half], [rrx.at[q, side, 3, half]])
            elif dist < 3:
                got(rrx.at[q, side, dist], rrx_rs.at[q, side, dist])
                add_into(dkv.at[q, j, k], [rrx.at[q, side, dist]])
        if dist == 0:
            got(rrx.at[q, 1, 0], rrx_rs.at[q, 1, 0])
            add_into(dkv.at[q, 0, k], [rrx.at[q, 1, 0]])
            return
        for side in (0, 1):
            j = j_of(side, dist)

            def make(j=j, side=side):
                if dist == 4:
                    half = pl.ds(side * 96, 96)
                    src, dst = dkv.at[q, 4, k, half], rrx.at[q, side, 3, half]
                else:
                    src, dst = dkv.at[q, j, k], rrx.at[q, side, dist - 1]
                return copy(src, dst, rrx_ss.at[q, side, dist - 1],
                            rrx_rs.at[q, side, dist - 1], ring[side])
            send(cond, make)

    def proj_pass(dist):
        for side in sides_of(dist):
            j = j_of(side, dist)
            slot = pj_slot(y, j, k)
            got(pjs.at[0, j], pjs_rs.at[0, j])
            got(pjy.at[j], pjy_rs.at[j])
            add_into(pj.at[slot], [pjs.at[0, j], pjy.at[j]])
            if dist == 3:
                half = pl.ds(side * 64, 64)
                got(pjr.at[side, 3, half], pjr_rs.at[side, 3])
                add_into(pj.at[slot, half], [pjr.at[side, 3, half]])
            elif dist < 3:
                got(pjr.at[side, dist], pjr_rs.at[side, dist])
                add_into(pj.at[slot], [pjr.at[side, dist]])
        if dist == 0:
            got(pjr.at[1, 0], pjr_rs.at[1, 0])
            add_into(pj.at[pj_slot(y, 0, k)], [pjr.at[1, 0]])
            return
        for side in (0, 1):
            j = j_of(side, dist)

            def make(j=j, side=side):
                if dist == 4:
                    half = pl.ds(side * 64, 64)
                    src, dst = pj.at[pj_slot(y, 4, k), half], pjr.at[side, 3, half]
                else:
                    src, dst = pj.at[pj_slot(y, j, k)], pjr.at[side, dist - 1]
                return copy(src, dst, pjr_ss.at[side, dist - 1],
                            pjr_rs.at[side, dist - 1], ring[side])
            send(None, make)

    def pass_on(dist):
        kv_pass(dist, 0, None)

        @pl.when(upper)
        def _():
            kv_pass(dist, 1, upper)

        proj_pass(dist)

    for dist in (4, 3, 2, 1, 0):
        backward_at(dist)
        if dist < 4:
            pass_on(dist + 1)

    query_rows = (dqt[...] * SCALE).T.astype(BF)
    empty = jnp.zeros((TOKENS - SLOTS, HEAD), BF)
    for h in range(HEADS):
        part = jnp.concatenate([query_rows[h * SLOTS:(h + 1) * SLOTS, :], empty], axis=0)
        qo_ref[:, h * HEAD:(h + 1) * HEAD] = mm(pickt[...], part).astype(BF)

    @pl.when(upper)
    def _():
        kv_pass(0, 1, upper)
        send(upper, lambda: copy(dkv.at[1, 0, k], yrx, yrx_s.at[0], yrx_s.at[1], across))

    kv_pass(0, 0, None)
    proj_pass(0)
    po_ref[...] = pj[pj_slot(y, 0, k)]

    @pl.when(lower)
    def _():
        got(yrx, yrx_s.at[1])
        add_into(dkv.at[0, 0, k], [yrx])

    sums = jnp.concatenate(
        [dkv[0, 0, k], jnp.zeros((TOKENS - SLOTS, 2 * HEAD), BF)], axis=0)
    kvo_ref[...] = mm(pickt[...], sums).astype(BF)

    for cond, make in pending:
        if cond is None:
            make().wait_send()
        else:
            @pl.when(cond)
            def _():
                make().wait_send()


def shards(queries, keys_values, upstream, out_proj, keep_index):
    keep = jnp.pad(keep_index, (0, TOKENS - SLOTS), constant_values=-1).reshape(1, TOKENS)
    dma = pltpu.SemaphoreType.DMA
    width = HEADS * HEAD
    vmem = pltpu.VMEM
    scratch = [
        vmem((4 * NZ, ROWS, 2 * HEAD), BF),
        vmem((4 * NZ, 128, width), BF),
        vmem((2 * NX, SLOTS, width), BF),
        vmem((2 * NZ, PAIR, QROWS), BF),
        vmem((2 * NZ, 8, QROWS), F32),
        vmem((QROWS, HEAD), BF),
        vmem((QROWS, HEAD), BF),
        vmem((HEAD, QROWS), F32),
        vmem((HEAD, QROWS), F32),
        vmem((8, QROWS), F32),
        vmem((TOKENS, TOKENS), BF),
        vmem((TOKENS, width), BF),
        vmem((SLOTS, width), F32),
        vmem((4 * NZ, 128, width), BF),
        vmem((2, NZ, 128, width), BF),
        vmem((NZ, 128, width), BF),
        vmem((2, 4, 128, width), BF),
        vmem((2, NZ, 2, SLOTS, 2 * HEAD), BF),
        vmem((2, NZ, SLOTS, 2 * HEAD), BF),
        vmem((2, 2, 4, SLOTS, 2 * HEAD), BF),
        vmem((SLOTS, 2 * HEAD), BF),
        dma((2, 2, 5)), dma((2, 2, 5)), dma((2, 2, 5)), dma((2, 2, 5)), dma((1,)),
        dma((2, 5)), dma((2, 5)), dma((2, 5)), dma((2, 5)),
        dma((2, 5)), dma((2, 5)), dma((2, 5)), dma((2, 5)),
        dma((2, 2, 3)), dma((2, 2, 3)),
        dma((2, NZ)), dma((2, NZ)), dma((NZ,)), dma((NZ,)), dma((2, 4)), dma((2, 4)),
        dma((2, NZ)), dma((2, NZ)), dma((2, 2, 4)), dma((2, 2, 4)), dma((2,)),
    ]
    return pl.pallas_call(
        kernel,
        out_shape=(
            jax.ShapeDtypeStruct(queries.shape, BF),
            jax.ShapeDtypeStruct(keys_values.shape, BF),
            jax.ShapeDtypeStruct(out_proj.shape, BF),
        ),
        in_specs=[pl.BlockSpec(memory_space=pltpu.VMEM)] * 5,
        out_specs=[pl.BlockSpec(memory_space=pltpu.VMEM)] * 3,
        scratch_shapes=scratch,
        compiler_params=pltpu.CompilerParams(
            collective_id=0, has_side_effects=True, vmem_limit_bytes=56 * 1024 * 1024
        ),
    )(keep, queries, keys_values, upstream, out_proj)


def solution(mesh):
    in_specs = (P("ctx", "tp"), P("ctx", "tp"), P("ctx", "tp"), P("ctx", "tp"), P("ctx"))
    out_specs = (P("ctx", "tp"), P("ctx", "tp"), P("ctx", "tp"))
    return jax.shard_map(shards, mesh=mesh, in_specs=in_specs, out_specs=out_specs, check_vma=False)
```

time: 541 us -> 98.8 us (0.18)
  waiting for transfers between devices: 332 us -> 0 us
  blocking collectives: 108 us -> 0 us
  Pallas kernels: 0 us -> 93.5 us
  loops' own time: 20.9 us -> 0 us
  matrix products: 20.5 us -> 0 us
  local copies, waits for them, and re-layouts: 22.8 us -> 4.56 us
  other arithmetic: 16.2 us -> 0 us
  between operations: 14.6 us -> 0.65 us
    unnamed x6 -> x0, waiting for transfers between devices: 149 us -> none
    reduce_scatter x1 -> x0, waiting for transfers between devices: 125 us -> none  [shards(): lax.psum_scatter(jnp.dot(column_list.T, attn_kept, preferred_element_type...]
    unnamed x1 -> x0, blocking collectives: 108 us -> none
    pallas_call x0 -> x1, Pallas kernels: none -> 93.5 us  [shards(): pl.pallas_call(kernel, out_shape=(jax.ShapeDtypeStruct(queries.shape, BF)...]
    all_gather x3 -> x0, waiting for transfers between devices: 58.6 us -> none  [the longest x1 58.5 us: shards(): lax.all_gather(out_proj, 'ctx', axis=0, tiled=True)]
    another operation x18 -> x0, loops' own time: 20.9 us -> none  [the longest x2 20.6 us: over_blocks(): return lax.fori_loop(0, piece_rows // block_width, one_block, carry)]
    dot_general x14 -> x0, matrix products: 20.5 us -> none  [the longest x3 4.64 us: compact(): jnp.dot(picker, matrix, preferred_element_type=jnp.float32)]
    reduce_min x16 -> x0, other arithmetic: 12.4 us -> none  [the longest x8 6.19 us: forward_step(): jnp.min(pos_block) <= newest]
  transfers between devices with their start and end apart: 5 -> 0, of which waited for: 3 -> 0; matrix products, arithmetic and copies ran while one was open for 5% -> 0% of each run, Pallas kernels for 0% -> 0%
where the time goes in v1:
time: 98.8 us; the launch traced here: 98.7 us
  Pallas kernels  93.5 us (95%)
  local copies, waits for them, and re-layouts  4.56 us (5%)
    pallas_call x1, Pallas kernels, shards(): pl.pallas_call(kernel, out_shape=(jax.ShapeDtypeStruct(queries.shape, BF)...  93.5 us
    unnamed x7, local copies, waits for them, and re-layouts  3.31 us

profile of v1, /device:TPU:1, one launch (start us, length us, event | category | flops | bytes accessed | tf_op | source)
XLA Modules:
  0.0 98.7 jit_solution(14012716735969152967)
XLA Ops:
  0.6 1.2 %pad.4 = s32[256]{0:T(256)} pad(s32[192]{0:T(256)} %param.9, s32[]{:T(128)} %constant.0.clone.1), padding=0_64 | pad | bytes 1796 | tf_op jit(solution)/shard_map/jit(_pad)/pad | solution.py:536
  1.9 93.5 %shard_map.76 = (bf16[256,512]{1,0:T(8,128)(2,1)}, bf16[256,256]{1,0:T(8,128)(2,1)}, bf16[128,512]{1,0:T(8,128)(2,1)}) custom-call(s32[1,256]{1,0:T(1,128)} %bitcast.1, bf16[256,512]{1,0:T(8,128)(2,1)} %q_ref.1, bf16[256,256]{1,0:T(8,128)(2,1)} %kv_ref.1, bf16[256,512]{1,0:T(8,128)(2,1)} %up_ref.1, bf16[128,512]{1,0:T(8,128)(2,1)} %w_ref.1), custom_call_target="tpu_custom_call" | custom-call | tf_op jit(solution)/shard_map/pallas_call | solution.py:569
  95.4 0.0 copy-start.1
  95.4 1.7 %copy.11 = bf16[256,512]{1,0:T(8,128)(2,1)} copy(bf16[256,512]{1,0:T(8,128)(2,1)} %get-tuple-element.6) | data formatting | bytes 524288
  97.1 0.0 copy-done.1
  97.1 0.0 copy-start
  97.1 0.7 copy.12
  97.7 0.3 copy-done
  98.0 0.7 copy.13
Async XLA Ops:
  95.4 1.7 %copy-start.1 = (bf16[256,256]{1,0:T(8,128)(2,1)S(1)}, bf16[256,256]{1,0:T(8,128)(2,1)}, u32[]{:S(2)}) copy-start(bf16[256,256]{1,0:T(8,128)(2,1)} %get-tuple-element.7) | copy-start | bytes 393220
  97.1 1.0 copy-start

commit v2 on v1

v2 whole, which is shorter than its diff:
```python
import functools
import math

import jax
import jax.numpy as jnp
from jax import lax
from jax.experimental import pallas as pl
from jax.experimental.pallas import tpu as pltpu
from jax.sharding import PartitionSpec as P

MESH = pl.DeviceIdType.MESH
BF = jnp.bfloat16
F32 = jnp.float32
NEG = -1e30
HEAD = 128
HEADS = 4
SLOTS = 192
ROWS = SLOTS + 16
PAIR = 2 * SLOTS
QROWS = HEADS * SLOTS
TOKENS = 256
NZ = 8
NX = 4
CHUNK = 256
SCALE = 1.0 / math.sqrt(HEAD)
LOG2 = SCALE * math.log2(math.e)
NT = (((1,), (1,)), ((), ()))


def mm(a, b):
    return jnp.dot(a, b, preferred_element_type=F32)


def kernel(
    keep_ref, q_ref, kv_ref, up_ref, w_ref,
    qo_ref, kvo_ref, po_ref,
    kvb, wb, ub, uown, eb, mb, qr, dor, ot, dqt, stat, pickt, attn, doacc, dsend, drecv, keeps,
    pj, pjs, pjr, dkv, sib, rrx, yvx, ykx,
    kv_rs, kv_ss, kvsib_rs, kvsib_ss, kvy_ss, vy_rs, vy_ss, vsib_rs, vsib_ss,
    w_rs, w_ss, wsib_rs, wsib_ss,
    u_rs, u_ss, uo_ss, do_s, at_s,
    pjs_rs, pjs_ss, pjr_rs, pjr_ss,
    sib_rs, sib_ss, rrx_rs, rrx_ss, yv_rs, yv_ss, yk_s,
):
    ctx = lax.axis_index("ctx")
    tp = lax.axis_index("tp")
    y = ctx // (2 * NZ)
    z = (ctx // 2) % NZ
    k = ctx % 2
    yh = tp // NX
    x = tp % NX

    def at_z(zz):
        return y * 2 * NZ + (zz % NZ) * 2 + k

    ring = ((at_z(z + 1), tp), (at_z(z + NZ - 1), tp))
    sibling = (ctx + 1 - 2 * k, tp)
    across = ((1 - y) * 2 * NZ + z * 2 + k, tp)
    xring = ((ctx, yh * NX + (x + 1) % NX), (ctx, yh * NX + (x + NX - 1) % NX))
    yh_peer = (ctx, (1 - yh) * NX + x)
    diagonal = (across[0], yh_peer[1])
    upper = y == 1
    lower = y == 0
    aligned = y == yh
    crossed = y != yh

    barrier = pltpu.get_barrier_semaphore()
    peers = ring + (sibling, across) + xring + (yh_peer, diagonal)
    for peer in peers:
        pl.semaphore_signal(barrier, inc=1, device_id=peer, device_id_type=MESH)

    pending = []

    def copy(src, dst, ssem, rsem, dev):
        return pltpu.make_async_remote_copy(
            src_ref=src, dst_ref=dst, send_sem=ssem, recv_sem=rsem,
            device_id=dev, device_id_type=MESH,
        )

    def send(cond, make):
        pending.append((cond, make))
        make().start()

    def got(ref, sem):
        copy(ref, ref, sem, sem, sibling).wait_recv()

    keeps[0:1, :] = jnp.full((1, TOKENS), -1, jnp.int32)
    keeps[0:1, 0:SLOTS] = keep_ref[...]
    keep = keeps[0:1, :]
    pick_t = jnp.where(
        lax.broadcasted_iota(jnp.int32, (TOKENS, TOKENS), 0) == keep, 1.0, 0.0
    ).astype(F32)
    pickt[...] = pick_t.astype(BF)
    pick = pick_t.T.astype(BF)[:SLOTS]
    count = jnp.sum(jnp.where(keep >= 0, 1.0, 0.0), axis=1, keepdims=True)
    kvb[ctx, 0:SLOTS, :] = mm(pick, kv_ref[...]).astype(BF)
    kvb[ctx, SLOTS:ROWS, :] = jnp.broadcast_to(count, (ROWS - SLOTS, 2 * HEAD)).astype(BF)
    wb[ctx % (2 * NZ)] = w_ref[...]
    uown[...] = mm(pick, up_ref[...]).astype(BF)

    @pl.when(aligned)
    def _():
        ub[x, 0] = uown[...]

    q_kept = mm(pick, q_ref[...]).astype(BF)
    for h in range(HEADS):
        qr[h * SLOTS:(h + 1) * SLOTS, :] = q_kept[:, h * HEAD:(h + 1) * HEAD]

    pl.semaphore_wait(barrier, len(peers))

    def slot_of(row, side, dist):
        zz = (z + NZ - dist) % NZ if side == 0 else (z + dist) % NZ
        return row * 2 * NZ + zz * 2 + k

    def kv_part(slot, side, dist, cols):
        if dist < 4:
            rows = pl.ds(0, ROWS)
        else:
            rows = pl.ds(0, 112) if side == 0 else pl.ds(112, 96)
        return kvb.at[slot, rows, cols]

    ALL, KEY, VALUE = pl.ds(0, 2 * HEAD), pl.ds(0, HEAD), pl.ds(HEAD, HEAD)

    def w_part(slot, side, dist):
        if dist < 4:
            return wb.at[slot]
        return wb.at[slot, pl.ds(side * 64, 64)]

    rows_of = (y, 0)
    cols_of = (ALL, KEY)

    def kv_ring(q, side, dist, cond=None):
        part = lambda: kv_part(slot_of(rows_of[q], side, dist), side, dist + 1, cols_of[q])
        send(cond, lambda: copy(
            part(), part(), kv_ss.at[q, side, dist], kv_rs.at[q, side, dist + 1], ring[side]))

    def kv_sib(q, side, dist, cond=None):
        part = lambda: kv_part(slot_of(rows_of[q], side, dist), side, dist, cols_of[q])
        send(cond, lambda: copy(
            part(), part(), kvsib_ss.at[q, side, dist], kvsib_rs.at[q, side, dist], sibling))

    def kv_sib_got(q, side, dist):
        slot = slot_of(rows_of[q], side, dist) + 1 - 2 * k
        got(kv_part(slot, side, dist, cols_of[q]), kvsib_rs.at[q, side, dist])

    def v_out(side, dist):
        part = lambda: kv_part(slot_of(0, side, dist), side, dist, VALUE)
        send(lower, lambda: copy(
            part(), part(), vy_ss.at[side, dist], vy_rs.at[side, dist], across))

    def v_across(side, dist):
        part = lambda: kv_part(slot_of(0, side, dist), side, dist, VALUE)
        got(part(), vy_rs.at[side, dist])
        send(upper, lambda: copy(
            part(), part(), vsib_ss.at[side, dist], vsib_rs.at[side, dist], sibling))

    def v_sib_got(side, dist):
        got(kv_part(slot_of(0, side, dist) + 1 - 2 * k, side, dist, VALUE), vsib_rs.at[side, dist])

    def w_ring(side, dist):
        part = lambda: w_part(slot_of(0, side, dist), side, dist + 1)
        send(None, lambda: copy(
            part(), part(), w_ss.at[side, dist], w_rs.at[side, dist + 1], ring[side]))

    def w_sib(side, dist):
        part = lambda: w_part(slot_of(0, side, dist), side, dist)
        send(None, lambda: copy(
            part(), part(), wsib_ss.at[side, dist], wsib_rs.at[side, dist], sibling))

    def w_sib_got(side, dist):
        got(w_part(slot_of(0, side, dist) + 1 - 2 * k, side, dist), wsib_rs.at[side, dist])

    def u_part(h, side, dist, half):
        xx = (x + NX - dist) % NX if side == 0 else (x + dist) % NX
        return ub.at[xx, h, pl.ds(side * 96, 96)] if half else ub.at[xx, h]

    def u_ring(h, side, dist):
        part = lambda: u_part(h, side, dist, dist + 1 == 2)
        send(None, lambda: copy(
            part(), part(), u_ss.at[h, side, dist], u_rs.at[h, side, dist + 1], xring[side]))

    def u_got(h, side, dist):
        got(u_part(h, side, dist, dist == 2), u_rs.at[h, side, dist])

    for side in (0, 1):
        w_ring(side, 0)
        kv_ring(0, side, 0)

    @pl.when(lower)
    def _():
        part = lambda: kvb.at[ctx, :, KEY]
        send(lower, lambda: copy(part(), part(), kvy_ss.at[0], kv_rs.at[1, 0, 0], across))
        v_out(0, 0)

    @pl.when(aligned)
    def _():
        send(aligned, lambda: copy(uown, ub.at[x, 0], uo_ss.at[0], u_rs.at[0, 0, 0], yh_peer))

    @pl.when(crossed)
    def _():
        send(crossed, lambda: copy(uown, ub.at[x, 1], uo_ss.at[0], u_rs.at[1, 0, 0], across))
        send(crossed, lambda: copy(uown, ub.at[x, 1], uo_ss.at[1], u_rs.at[1, 0, 0], diagonal))

    kv_sib(0, 0, 0)
    w_sib(0, 0)

    ot[...] = jnp.zeros_like(ot)
    dqt[...] = jnp.zeros_like(dqt)
    stat[0:1, :] = jnp.full((1, QROWS), NEG, F32)
    stat[1:2, :] = jnp.zeros((1, QROWS), F32)

    def load_pair(p):
        block = kvb[pl.ds(2 * p, 2), 0:SLOTS, :]
        return (block[:, :, 0:HEAD].reshape(PAIR, HEAD), block[:, :, HEAD:].reshape(PAIR, HEAD))

    def turned(block):
        return block.astype(F32).T.astype(BF)

    def forward_block(p, own):
        keys, values = load_pair(p)
        values_t = turned(values)
        counts = kvb[pl.ds(2 * p, 2), SLOTS:ROWS, 0:HEAD].astype(F32)
        place = lax.broadcasted_iota(jnp.int32, (SLOTS, HEAD), 0).astype(F32)
        bias = jnp.concatenate(
            [jnp.where(place < counts[i, 0:1, :], 0.0, NEG) for i in (0, 1)], axis=0)
        bias = jnp.concatenate([bias] * (CHUNK // HEAD), axis=1)
        for first in range(0, QROWS, CHUNK):
            cols = slice(first, first + CHUNK)
            scores = lax.dot_general(keys, qr[cols, :], NT, preferred_element_type=F32) + bias
            if own:
                row = lax.broadcasted_iota(jnp.int32, (SLOTS, CHUNK), 0)
                col = (lax.broadcasted_iota(jnp.int32, (SLOTS, CHUNK), 1) + first) % SLOTS
                late = jnp.concatenate(
                    [jnp.where(row - col <= (k - i) * 1024, 0.0, NEG) for i in (0, 1)], axis=0)
                scores = scores + late
            old = stat[0:1, cols]
            new = jnp.maximum(old, jnp.max(scores, axis=0, keepdims=True) * LOG2)
            weights = jnp.exp2(scores * LOG2 - new)
            shrink = jnp.exp2(old - new)
            stat[0:1, cols] = new
            stat[1:2, cols] = stat[1:2, cols] * shrink + jnp.sum(weights, axis=0, keepdims=True)
            half = weights.astype(BF)
            eb[p, :, cols] = half
            mb[p, 0:1, cols] = new
            ot[:, cols] = ot[:, cols] * shrink + mm(values_t, half)

    kv_sib_got(0, 0, 0)
    forward_block(y * NZ + z, True)

    @pl.when(upper)
    def _():
        got(kvb.at[slot_of(0, 0, 0), :, KEY], kv_rs.at[1, 0, 0])
        for side in (0, 1):
            kv_ring(1, side, 0, upper)
        kv_sib(1, 0, 0, upper)
        v_across(0, 0)

    @pl.when(crossed)
    def _():
        got(ub.at[x, 0], u_rs.at[0, 0, 0])

    for side in (0, 1):
        u_ring(0, side, 0)

    def forward_at(dist):
        sides = (0, 1) if 0 < dist < 4 else (0,)
        halves = (0, 1) if dist > 0 else (0,)

        @pl.when(upper)
        def _():
            for side in halves:
                if dist > 0:
                    v_across(side, dist)

        if dist > 0:
            for side in halves:
                kv_sib_got(0, side, dist)

        def blocks(q):
            def step(side, carry):
                zz = (z + jnp.where(side == 0, NZ - dist, dist)) % NZ
                if q == 1:
                    forward_block(zz, False)
                else:
                    @pl.when(zz < z)
                    def _():
                        forward_block(y * NZ + zz, False)
                return carry

            lax.fori_loop(0, len(sides), step, 0)

        if dist > 0:
            blocks(0)

        @pl.when(upper)
        def _():
            for side in halves:
                kv_sib_got(1, side, dist)
                v_sib_got(side, dist)
            blocks(1)

    for dist in range(1, 5):
        for side in (0, 1):
            got(w_part(slot_of(0, side, dist), side, dist), w_rs.at[side, dist])
            if dist < 4:
                w_ring(side, dist)
            w_sib(side, dist)
            got(kv_part(slot_of(y, side, dist), side, dist, ALL), kv_rs.at[0, side, dist])
            if dist < 4:
                kv_ring(0, side, dist)
            kv_sib(0, side, dist)

        @pl.when(lower)
        def _():
            for side in (0, 1):
                v_out(side, dist)

        @pl.when(upper)
        def _():
            for side in (0, 1):
                got(kv_part(slot_of(0, side, dist), side, dist, KEY), kv_rs.at[1, side, dist])
                if dist < 4:
                    kv_ring(1, side, dist, upper)
                kv_sib(1, side, dist, upper)

        if dist == 1:
            got(ub.at[x, 1], u_rs.at[1, 0, 0])
            for side in (0, 1):
                u_ring(1, side, 0)
            for side in (0, 1):
                u_got(0, side, 1)
                u_ring(0, side, 1)
        if dist == 2:
            for side in (0, 1):
                u_got(1, side, 1)
                u_ring(1, side, 1)
        forward_at(dist - 1)

    for h in (0, 1):
        for side in (0, 1):
            u_got(h, side, 2)
    for dist in range(0, 5):
        for side in ((0, 1) if dist > 0 else (0,)):
            w_sib_got(side, dist)
    doacc[...] = jnp.zeros_like(doacc)

    def head_grads(i, carry):
        doacc[...] += mm(ub[i].reshape(PAIR, HEADS * HEAD),
                         wb[pl.ds(4 * i, 4)].reshape(4 * 128, HEADS * HEAD))
        return carry

    lax.fori_loop(0, NX, head_grads, 0)
    dsend[...] = doacc[SLOTS:, :].astype(BF)
    send(None, lambda: copy(dsend, drecv, do_s.at[0], do_s.at[1], across))

    forward_at(4)

    total = stat[1:2, :]
    inv = 1.0 / total
    stat[1:2, :] = inv
    attn_t = (ot[...] * inv).astype(BF).astype(F32)
    ot[...] = attn_t
    attn_rows = attn_t.T.astype(BF)
    for h in range(HEADS):
        attn[0, :, h * HEAD:(h + 1) * HEAD] = attn_rows[h * SLOTS:(h + 1) * SLOTS, :]
    send(None, lambda: copy(attn.at[0], attn.at[1], at_s.at[0], at_s.at[1], across))

    got(drecv, do_s.at[1])
    for h in range(HEADS):
        cols = slice(h * HEAD, (h + 1) * HEAD)
        grads = (doacc[0:SLOTS, cols] + drecv[:, cols].astype(F32)).astype(BF)
        dor[h * SLOTS:(h + 1) * SLOTS, :] = grads
    stat[2:3, :] = jnp.sum(dor[...].astype(F32).T * ot[...], axis=0, keepdims=True)

    def pj_slot(j, core):
        return ((z + j) % NZ) * 2 + core

    def proj_terms():
        got(attn.at[1], at_s.at[1])

        def step(i, carry):
            block = ub[i].reshape(PAIR, HEADS * HEAD).astype(F32)
            term = mm(block.T.astype(BF), attn[...].reshape(PAIR, HEADS * HEAD)).astype(BF)
            pj[pl.ds(4 * i, 4)] = term.reshape(4, 128, HEADS * HEAD)
            return carry

        lax.fori_loop(0, NX, step, 0)
        for j in (4, 3, 5, 2, 6, 1, 7, 0):
            send(None, lambda j=j: copy(
                pj.at[pj_slot(j, 1 - k)], pjs.at[j], pjs_ss.at[j], pjs_rs.at[j], sibling))

    def backward_block(p, q, j):
        keys, values = load_pair(p)
        keys_t = turned(keys)
        key_grad = jnp.zeros((PAIR, HEAD), F32)
        value_grad = jnp.zeros((PAIR, HEAD), F32)
        for first in range(0, QROWS, CHUNK):
            cols = slice(first, first + CHUNK)
            level = jnp.exp2(mb[p, 0:1, cols] - stat[0:1, cols]) * stat[1:2, cols]
            probs = eb[p, :, cols].astype(F32) * level
            grads = dor[cols, :]
            value_grad = value_grad + mm(probs.astype(BF), grads)
            pushes = lax.dot_general(values, grads, NT, preferred_element_type=F32)
            slopes = (probs * (pushes - stat[2:3, cols])).astype(BF)
            key_grad = key_grad + mm(slopes, qr[cols, :])
            dqt[:, cols] += mm(keys_t, slopes)
        dkv[q, j, :, :, 0:HEAD] = (key_grad * SCALE).astype(BF).reshape(2, SLOTS, HEAD)
        dkv[q, j, :, :, HEAD:] = value_grad.astype(BF).reshape(2, SLOTS, HEAD)

    def sides_of(dist):
        return (0, 1) if 0 < dist < 4 else (0,)

    def j_of(side, dist):
        return dist if side == 0 else NZ - dist

    def backward_at(dist):
        sides = sides_of(dist)

        def blocks(q):
            def step(side, carry):
                j = jnp.where(side == 0, dist, (NZ - dist) % NZ)
                zz = (z + j) % NZ
                if q == 1:
                    backward_block(zz, q, j)
                else:
                    @pl.when(zz <= z)
                    def _():
                        backward_block(y * NZ + zz, q, j)

                    @pl.when(zz > z)
                    def _():
                        dkv[q, j] = jnp.zeros((2, SLOTS, 2 * HEAD), BF)
                return carry

            lax.fori_loop(0, len(sides), step, 0)

        def swap(q, cond):
            for side in sides:
                j = j_of(side, dist)
                send(cond, lambda j=j: copy(
                    dkv.at[q, j, 1 - k], sib.at[q, j], sib_ss.at[q, j], sib_rs.at[q, j], sibling))

        @pl.when(upper)
        def _():
            blocks(1)
            swap(1, upper)

        blocks(0)
        swap(0, None)

    def add_into(ref, parts):
        value = ref[...].astype(F32)
        for part in parts:
            value = value + part[...].astype(F32)
        ref[...] = value.astype(BF)

    def kv_pass(dist, q, cond):
        cols = cols_of[q]
        for side in sides_of(dist):
            j = j_of(side, dist)
            got(sib.at[q, j], sib_rs.at[q, j])
            add_into(dkv.at[q, j, k], [sib.at[q, j]])
            if q == 1:
                send(upper, lambda j=j: copy(
                    dkv.at[1, j, k, :, VALUE], yvx.at[j], yv_ss.at[j], yv_rs.at[j], across))
            else:
                @pl.when(lower)
                def _():
                    got(yvx.at[j], yv_rs.at[j])
                    add_into(dkv.at[0, j, k, :, VALUE], [yvx.at[j]])
            if dist == 3:
                half = pl.ds(side * 96, 96)
                part = rrx.at[q, side, 3, half, cols]
                got(part, rrx_rs.at[q, side, 3])
                add_into(dkv.at[q, j, k, half, cols], [part])
            elif dist < 3:
                part = rrx.at[q, side, dist, :, cols]
                got(part, rrx_rs.at[q, side, dist])
                add_into(dkv.at[q, j, k, :, cols], [part])
        if dist == 0:
            part = rrx.at[q, 1, 0, :, cols]
            got(part, rrx_rs.at[q, 1, 0])
            add_into(dkv.at[q, 0, k, :, cols], [part])
            return
        for side in (0, 1):
            def make(side=side):
                if dist == 4:
                    half = pl.ds(side * 96, 96)
                    src, dst = dkv.at[q, 4, k, half, cols], rrx.at[q, side, 3, half, cols]
                else:
                    src = dkv.at[q, j_of(side, dist), k, :, cols]
                    dst = rrx.at[q, side, dist - 1, :, cols]
                return copy(src, dst, rrx_ss.at[q, side, dist - 1],
                            rrx_rs.at[q, side, dist - 1], ring[side])
            send(cond, make)

    def proj_pass(dist):
        for side in sides_of(dist):
            j = j_of(side, dist)
            slot = pj_slot(j, k)
            got(pjs.at[j], pjs_rs.at[j])
            parts = [pjs.at[j]]
            if 0 < dist < 3:
                got(pjr.at[side, dist], pjr_rs.at[side, dist])
                parts.append(pjr.at[side, dist])
            elif dist == 0:
                for other in (0, 1):
                    got(pjr.at[other, 0], pjr_rs.at[other, 0])
                    parts.append(pjr.at[other, 0])
            add_into(pj.at[slot], parts)
            if dist == 3:
                half = pl.ds(side * 64, 64)
                got(pjr.at[side, 3, half], pjr_rs.at[side, 3])
                add_into(pj.at[slot, half], [pjr.at[side, 3, half]])
        if dist == 0:
            return
        for side in (0, 1):
            def make(side=side):
                if dist == 4:
                    half = pl.ds(side * 64, 64)
                    src, dst = pj.at[pj_slot(4, k), half], pjr.at[side, 3, half]
                else:
                    src, dst = pj.at[pj_slot(j_of(side, dist), k)], pjr.at[side, dist - 1]
                return copy(src, dst, pjr_ss.at[side, dist - 1],
                            pjr_rs.at[side, dist - 1], ring[side])
            send(None, make)

    def pass_on(dist):
        @pl.when(upper)
        def _():
            kv_pass(dist, 1, upper)

        proj_pass(dist)
        kv_pass(dist, 0, None)

    for dist in (4, 3, 2, 1, 0):
        backward_at(dist)
        if dist == 4:
            proj_terms()
        else:
            pass_on(dist + 1)

    query_rows = (dqt[...] * SCALE).T.astype(BF)
    empty = jnp.zeros((TOKENS - SLOTS, HEAD), BF)
    for h in range(HEADS):
        part = jnp.concatenate([query_rows[h * SLOTS:(h + 1) * SLOTS, :], empty], axis=0)
        qo_ref[:, h * HEAD:(h + 1) * HEAD] = mm(pickt[...], part).astype(BF)

    @pl.when(upper)
    def _():
        kv_pass(0, 1, upper)
        send(upper, lambda: copy(
            dkv.at[1, 0, k, :, KEY], ykx, yk_s.at[0], yk_s.at[1], across))

    proj_pass(0)
    po_ref[...] = pj[pj_slot(0, k)]
    kv_pass(0, 0, None)

    @pl.when(lower)
    def _():
        got(ykx, yk_s.at[1])
        add_into(dkv.at[0, 0, k, :, KEY], [ykx])

    sums = jnp.concatenate(
        [dkv[0, 0, k], jnp.zeros((TOKENS - SLOTS, 2 * HEAD), BF)], axis=0)
    kvo_ref[...] = mm(pickt[...], sums).astype(BF)

    for cond, make in pending:
        if cond is None:
            make().wait_send()
        else:
            @pl.when(cond)
            def _():
                make().wait_send()


def shards(queries, keys_values, upstream, out_proj, keep_index):
    keep = keep_index.reshape(1, SLOTS)
    dma = pltpu.SemaphoreType.DMA
    width = HEADS * HEAD
    vmem = pltpu.VMEM
    scratch = [
        vmem((4 * NZ, ROWS, 2 * HEAD), BF),
        vmem((2 * NZ, 128, width), BF),
        vmem((NX, 2, SLOTS, width), BF),
        vmem((SLOTS, width), BF),
        vmem((2 * NZ, PAIR, QROWS), BF),
        vmem((2 * NZ, 8, QROWS), F32),
        vmem((QROWS, HEAD), BF),
        vmem((QROWS, HEAD), BF),
        vmem((HEAD, QROWS), F32),
        vmem((HEAD, QROWS), F32),
        vmem((8, QROWS), F32),
        vmem((TOKENS, TOKENS), BF),
        vmem((2, SLOTS, width), BF),
        vmem((PAIR, width), F32),
        vmem((SLOTS, width), BF),
        vmem((SLOTS, width), BF),
        vmem((8, TOKENS), jnp.int32),
        vmem((2 * NZ, 128, width), BF),
        vmem((NZ, 128, width), BF),
        vmem((2, 4, 128, width), BF),
        vmem((2, NZ, 2, SLOTS, 2 * HEAD), BF),
        vmem((2, NZ, SLOTS, 2 * HEAD), BF),
        vmem((2, 2, 4, SLOTS, 2 * HEAD), BF),
        vmem((NZ, SLOTS, HEAD), BF),
        vmem((SLOTS, HEAD), BF),
        dma((2, 2, 5)), dma((2, 2, 5)), dma((2, 2, 5)), dma((2, 2, 5)), dma((1,)),
        dma((2, 5)), dma((2, 5)), dma((2, 5)), dma((2, 5)),
        dma((2, 5)), dma((2, 5)), dma((2, 5)), dma((2, 5)),
        dma((2, 2, 3)), dma((2, 2, 3)), dma((2,)), dma((2,)), dma((2,)),
        dma((NZ,)), dma((NZ,)), dma((2, 4)), dma((2, 4)),
        dma((2, NZ)), dma((2, NZ)), dma((2, 2, 4)), dma((2, 2, 4)),
        dma((NZ,)), dma((NZ,)), dma((2,)),
    ]
    return pl.pallas_call(
        kernel,
        out_shape=(
            jax.ShapeDtypeStruct(queries.shape, BF),
            jax.ShapeDtypeStruct(keys_values.shape, BF),
            jax.ShapeDtypeStruct(out_proj.shape, BF),
        ),
        in_specs=[pl.BlockSpec(memory_space=pltpu.VMEM)] * 5,
        out_specs=[pl.BlockSpec(memory_space=pltpu.VMEM)] * 3,
        scratch_shapes=scratch,
        compiler_params=pltpu.CompilerParams(
            collective_id=0, has_side_effects=True, vmem_limit_bytes=56 * 1024 * 1024
        ),
    )(keep, queries, keys_values, upstream, out_proj)


def solution(mesh):
    in_specs = (P("ctx", "tp"), P("ctx", "tp"), P("ctx", "tp"), P("ctx", "tp"), P("ctx"))
    out_specs = (P("ctx", "tp"), P("ctx", "tp"), P("ctx", "tp"))
    return jax.shard_map(shards, mesh=mesh, in_specs=in_specs, out_specs=out_specs, check_vma=False)
```

time: 98.8 us -> 85.6 us (0.87); the launches traced: 98.7 us -> 83.9 us
  Pallas kernels: 93.5 us -> 79.9 us
  local copies, waits for them, and re-layouts: 4.56 us -> 3.31 us
    pallas_call x1, Pallas kernels: 93.5 us -> 79.9 us  [shards(): pl.pallas_call(kernel, out_shape=(jax.ShapeDtypeStruct(queries.shape, BF)...]
    pad x1 -> x0, local copies, waits for them, and re-layouts: 1.24 us -> none  [shards(): jnp.pad(keep_index, (0, TOKENS - SLOTS), constant_values=-1)]
where the time goes in v2:
time: 85.6 us; the launch traced here: 83.9 us
  Pallas kernels  79.9 us (93%)
  local copies, waits for them, and re-layouts  3.31 us (4%)
    pallas_call x1, Pallas kernels, shards(): pl.pallas_call(kernel, out_shape=(jax.ShapeDtypeStruct(queries.shape, BF)...  79.9 us
    unnamed x7, local copies, waits for them, and re-layouts  3.31 us

profile of v2, /device:TPU:1, one launch (start us, length us, event | category | flops | bytes accessed | tf_op | source)
XLA Modules:
  0.0 83.9 jit_solution(16313009377765040413)
XLA Ops:
  0.6 79.9 %shard_map.76 = (bf16[256,512]{1,0:T(8,128)(2,1)}, bf16[256,256]{1,0:T(8,128)(2,1)}, bf16[128,512]{1,0:T(8,128)(2,1)}) custom-call(s32[1,192]{1,0:T(1,128)} %bitcast.1, bf16[256,512]{1,0:T(8,128)(2,1)} %q_ref.1, bf16[256,256]{1,0:T(8,128)(2,1)} %kv_ref.1, bf16[256,512]{1,0:T(8,128)(2,1)} %up_ref.1, bf16[128,512]{1,0:T(8,128)(2,1)} %w_ref.1), custom_call_target="tpu_custom_call" | custom-call | tf_op jit(solution)/shard_map/pallas_call | solution.py:616
  80.6 0.0 copy-start.1
  80.6 1.7 %copy.11 = bf16[256,512]{1,0:T(8,128)(2,1)} copy(bf16[256,512]{1,0:T(8,128)(2,1)} %get-tuple-element.6) | data formatting | bytes 524288
  82.3 0.0 copy-done.1
  82.3 0.0 copy-start
  82.3 0.7 copy.12
  82.9 0.3 copy-done
  83.2 0.7 copy.13
Async XLA Ops:
  80.6 1.7 %copy-start.1 = (bf16[256,256]{1,0:T(8,128)(2,1)S(1)}, bf16[256,256]{1,0:T(8,128)(2,1)}, u32[]{:S(2)}) copy-start(bf16[256,256]{1,0:T(8,128)(2,1)} %get-tuple-element.7) | copy-start | bytes 393220
  82.3 1.0 %copy-start = (bf16[128,512]{1,0:T(8,128)(2,1)S(1)}, bf16[128,512]{1,0:T(8,128)(2,1)}, u32[]{:S(2)}) copy-start(bf16[128,512]{1,0:T(8,128)(2,1)} %get-tuple-element.8) | copy-start | bytes 393220

commit v3 on v2

v3 whole, which is shorter than its diff:
```python
import functools
import math

import jax
import jax.numpy as jnp
from jax import lax
from jax.experimental import pallas as pl
from jax.experimental.pallas import tpu as pltpu
from jax.sharding import PartitionSpec as P

MESH = pl.DeviceIdType.MESH
BF = jnp.bfloat16
F32 = jnp.float32
NEG = -1e30
HEAD = 128
HEADS = 4
SLOTS = 192
ROWS = SLOTS + 16
PAIR = 2 * SLOTS
QROWS = HEADS * SLOTS
TOKENS = 256
CHUNK = 256
NZ = 8
NX = 4
SCALE = 1.0 / math.sqrt(HEAD)
LOG2 = SCALE * math.log2(math.e)
NT = (((1,), (1,)), ((), ()))


def mm(a, b):
    return jnp.dot(a, b, preferred_element_type=F32)


def kernel(
    keep_ref, q_ref, kv_ref, up_ref, w_ref,
    qo_ref, kvo_ref, po_ref,
    kvb, wb, ub, uown, eb, mb, qr, dor, ot, dqt, stat, pickt, attn, doacc, dsend, drecv, keeps,
    pj, pjs, pjr, dkv, sib, rrx, yvx,
    kv_rs, kv_ss, kvsib_rs, kvsib_ss, vy_rs, vy_ss, vsib_rs, vsib_ss,
    w_rs, w_ss, wsib_rs, wsib_ss,
    u_rs, u_ss, uo_ss, do_s, at_s,
    pjs_rs, pjs_ss, pjr_rs, pjr_ss,
    sib_rs, sib_ss, rrx_rs, rrx_ss, yv_rs, yv_ss,
):
    ctx = lax.axis_index("ctx")
    tp = lax.axis_index("tp")
    y = ctx // (2 * NZ)
    z = (ctx // 2) % NZ
    k = ctx % 2
    yh = tp // NX
    x = tp % NX

    def at_z(zz):
        return y * 2 * NZ + (zz % NZ) * 2 + k

    ring = ((at_z(z + 1), tp), (at_z(z + NZ - 1), tp))
    sibling = (ctx + 1 - 2 * k, tp)
    across = ((1 - y) * 2 * NZ + z * 2 + k, tp)
    xring = ((ctx, yh * NX + (x + 1) % NX), (ctx, yh * NX + (x + NX - 1) % NX))
    yh_peer = (ctx, (1 - yh) * NX + x)
    diagonal = (across[0], yh_peer[1])
    upper = y == 1
    lower = y == 0
    aligned = y == yh
    crossed = y != yh

    barrier = pltpu.get_barrier_semaphore()
    peers = ring + (sibling, across) + xring + (yh_peer, diagonal)
    for peer in peers:
        pl.semaphore_signal(barrier, inc=1, device_id=peer, device_id_type=MESH)

    pending = []

    def copy(src, dst, ssem, rsem, dev):
        return pltpu.make_async_remote_copy(
            src_ref=src, dst_ref=dst, send_sem=ssem, recv_sem=rsem,
            device_id=dev, device_id_type=MESH,
        )

    def send(cond, make):
        pending.append((cond, make))
        make().start()

    def got(ref, sem):
        copy(ref, ref, sem, sem, sibling).wait_recv()

    keeps[0:1, :] = jnp.full((1, TOKENS), -1, jnp.int32)
    keeps[0:1, 0:SLOTS] = keep_ref[...]
    keep = keeps[0:1, :]
    pick_t = jnp.where(
        lax.broadcasted_iota(jnp.int32, (TOKENS, TOKENS), 0) == keep, 1.0, 0.0
    ).astype(F32)
    pickt[...] = pick_t.astype(BF)
    pick = pick_t.T.astype(BF)[:SLOTS]
    count = jnp.sum(jnp.where(keep >= 0, 1.0, 0.0), axis=1, keepdims=True)
    kvb[ctx, 0:SLOTS, :] = mm(pick, kv_ref[...]).astype(BF)
    kvb[ctx, SLOTS:ROWS, :] = jnp.broadcast_to(count, (ROWS - SLOTS, 2 * HEAD)).astype(BF)
    uown[...] = mm(pick, up_ref[...]).astype(BF)
    wb[ctx % (2 * NZ)] = w_ref[...]

    @pl.when(aligned)
    def _():
        ub[x, 0] = uown[...]

    pl.semaphore_wait(barrier, len(peers))

    def slot_of(row, side, dist):
        zz = (z + NZ - dist) % NZ if side == 0 else (z + dist) % NZ
        return row * 2 * NZ + zz * 2 + k

    def kv_part(slot, side, dist, cols):
        if dist < 4:
            rows = pl.ds(0, ROWS)
        else:
            rows = pl.ds(0, 112) if side == 0 else pl.ds(112, 96)
        return kvb.at[slot, rows, cols]

    ALL, KEY, VALUE = pl.ds(0, 2 * HEAD), pl.ds(0, HEAD), pl.ds(HEAD, HEAD)

    def w_part(slot, side, dist):
        if dist < 4:
            return wb.at[slot]
        return wb.at[slot, pl.ds(side * 64, 64)]

    rows_of = (y, 0)
    cols_of = (ALL, KEY)

    def kv_ring(q, side, dist, cond=None):
        part = lambda: kv_part(slot_of(rows_of[q], side, dist), side, dist + 1, cols_of[q])
        send(cond, lambda: copy(
            part(), part(), kv_ss.at[q, side, dist], kv_rs.at[q, side, dist + 1], ring[side]))

    def kv_sib(q, side, dist, cond=None):
        part = lambda: kv_part(slot_of(rows_of[q], side, dist), side, dist, cols_of[q])
        send(cond, lambda: copy(
            part(), part(), kvsib_ss.at[q, side, dist], kvsib_rs.at[q, side, dist], sibling))

    def kv_sib_got(q, side, dist):
        slot = slot_of(rows_of[q], side, dist) + 1 - 2 * k
        got(kv_part(slot, side, dist, cols_of[q]), kvsib_rs.at[q, side, dist])

    def across_cols(dist):
        return VALUE if dist == 1 else ALL

    def v_out(side, dist):
        part = lambda: kv_part(slot_of(0, side, dist), side, dist, across_cols(dist))
        send(lower, lambda: copy(
            part(), part(), vy_ss.at[side, dist], vy_rs.at[side, dist], across))

    def v_across(side, dist):
        part = lambda: kv_part(slot_of(0, side, dist), side, dist, across_cols(dist))
        got(part(), vy_rs.at[side, dist])
        send(upper, lambda: copy(
            part(), part(), vsib_ss.at[side, dist], vsib_rs.at[side, dist], sibling))

    def v_sib_got(side, dist):
        slot = slot_of(0, side, dist) + 1 - 2 * k
        got(kv_part(slot, side, dist, across_cols(dist)), vsib_rs.at[side, dist])

    def w_ring(side, dist):
        part = lambda: w_part(slot_of(0, side, dist), side, dist + 1)
        send(None, lambda: copy(
            part(), part(), w_ss.at[side, dist], w_rs.at[side, dist + 1], ring[side]))

    def w_sib(side, dist):
        part = lambda: w_part(slot_of(0, side, dist), side, dist)
        send(None, lambda: copy(
            part(), part(), wsib_ss.at[side, dist], wsib_rs.at[side, dist], sibling))

    def w_sib_got(side, dist):
        got(w_part(slot_of(0, side, dist) + 1 - 2 * k, side, dist), wsib_rs.at[side, dist])

    def u_part(h, side, dist, half):
        xx = (x + NX - dist) % NX if side == 0 else (x + dist) % NX
        return ub.at[xx, h, pl.ds(side * 96, 96)] if half else ub.at[xx, h]

    def u_ring(h, side, dist, cond=None):
        part = lambda: u_part(h, side, dist, dist + 1 == 2)
        send(cond, lambda: copy(
            part(), part(), u_ss.at[h, side, dist], u_rs.at[h, side, dist + 1], xring[side]))

    def u_got(h, side, dist):
        got(u_part(h, side, dist, dist == 2), u_rs.at[h, side, dist])

    for side in (0, 1):
        kv_ring(0, side, 0)

    @pl.when(aligned)
    def _():
        send(aligned, lambda: copy(uown, ub.at[x, 0], uo_ss.at[0], u_rs.at[0, 0, 0], yh_peer))

    @pl.when(crossed)
    def _():
        send(crossed, lambda: copy(uown, ub.at[x, 1], uo_ss.at[0], u_rs.at[1, 0, 0], across))
        send(crossed, lambda: copy(uown, ub.at[x, 1], uo_ss.at[1], u_rs.at[1, 0, 0], diagonal))

    @pl.when(aligned)
    def _():
        for side in (0, 1):
            u_ring(0, side, 0, aligned)

    kv_sib(0, 0, 0)

    @pl.when(lower)
    def _():
        v_out(0, 0)

    q_kept = mm(pick, q_ref[...]).astype(BF)
    for h in range(HEADS):
        qr[h * SLOTS:(h + 1) * SLOTS, :] = q_kept[:, h * HEAD:(h + 1) * HEAD]

    ot[...] = jnp.zeros_like(ot)
    dqt[...] = jnp.zeros_like(dqt)
    stat[0:1, :] = jnp.full((1, QROWS), NEG, F32)
    stat[1:2, :] = jnp.zeros((1, QROWS), F32)

    def load_pair(p):
        block = kvb[pl.ds(2 * p, 2), 0:SLOTS, :]
        return (block[:, :, 0:HEAD].reshape(PAIR, HEAD), block[:, :, HEAD:].reshape(PAIR, HEAD))

    def turned(block):
        return block.astype(F32).T.astype(BF)

    def key_bias(p):
        counts = kvb[pl.ds(2 * p, 2), SLOTS:ROWS, 0:HEAD].astype(F32)
        place = lax.broadcasted_iota(jnp.int32, (SLOTS, HEAD), 0).astype(F32)
        bias = jnp.concatenate(
            [jnp.where(place < counts[i, 0:1, :], 0.0, NEG) for i in (0, 1)], axis=0)
        return jnp.concatenate([bias] * (CHUNK // HEAD), axis=1)

    def forward_blocks(pairs, own=False):
        loaded = [load_pair(p) for p in pairs]
        biases = [key_bias(p) for p in pairs]
        values_t = jnp.concatenate([turned(values) for _, values in loaded], axis=1)
        values_t = jnp.concatenate(
            [values_t, jnp.ones((16, PAIR * len(pairs)), BF)], axis=0)
        old = stat[0:1, :]
        maxima, halves = [], []
        for first in range(0, QROWS, CHUNK):
            cols = slice(first, first + CHUNK)
            new = old[:, cols]
            scores = []
            for (keys, _), bias in zip(loaded, biases):
                part = lax.dot_general(keys, qr[cols, :], NT, preferred_element_type=F32)
                part = part * LOG2 + bias
                if own:
                    row = lax.broadcasted_iota(jnp.int32, (SLOTS, CHUNK), 0)
                    col = (lax.broadcasted_iota(jnp.int32, (SLOTS, CHUNK), 1) + first) % SLOTS
                    part = part + jnp.concatenate(
                        [jnp.where(row - col <= (k - i) * 1024, 0.0, NEG) for i in (0, 1)], axis=0)
                scores.append(part)
                new = jnp.maximum(new, jnp.max(part, axis=0, keepdims=True))
            weights = [jnp.exp2(part - new).astype(BF) for part in scores]
            for p, part in zip(pairs, weights):
                eb[p, :, cols] = part
                mb[p, 0:1, cols] = new
            halves.append(jnp.concatenate(weights, axis=0))
            maxima.append(new)
        new = jnp.concatenate(maxima, axis=1)
        shrink = jnp.exp2(old - new)
        sums = mm(values_t, jnp.concatenate(halves, axis=1))
        ot[...] = ot[...] * shrink + sums[0:HEAD]
        stat[0:1, :] = new
        stat[1:2, :] = stat[1:2, :] * shrink + sums[HEAD:HEAD + 1]

    kv_sib_got(0, 0, 0)
    forward_blocks([y * NZ + z], True)

    for side in (0, 1):
        w_ring(side, 0)
    w_sib(0, 0)

    def sides_of(dist):
        return (0, 1) if 0 < dist < 4 else (0,)

    def chip_at(j):
        return (z + j) % NZ

    def forward_own_row(dist):
        for side in (0, 1):
            kv_sib_got(0, side, dist)
        before, behind = y * NZ + chip_at(NZ - dist), y * NZ + chip_at(dist)
        near, far = z >= dist, z + dist >= NZ

        @pl.when(jnp.logical_and(near, far))
        def _():
            forward_blocks([before, behind])

        @pl.when(near != far)
        def _():
            forward_blocks([jnp.where(near, before, behind)])

    def forward_other_row(dist):
        @pl.when(upper)
        def _():
            for side in ((0, 1) if dist > 0 else (0,)):
                if dist == 1:
                    kv_sib_got(1, side, dist)
                v_sib_got(side, dist)
            forward_blocks([chip_at(NZ - dist), chip_at(dist)] if dist > 0 else [z])

    def forward_opposite():
        for side in (0, 1):
            kv_sib_got(0, side, 4)
        there = chip_at(4)

        @pl.when(upper)
        def _():
            for side in (0, 1):
                v_sib_got(side, 4)

        @pl.when(jnp.logical_and(upper, z >= 4))
        def _():
            forward_blocks([there, y * NZ + there])

        @pl.when(upper != (z >= 4))
        def _():
            forward_blocks([there])

    def other_row_got(dist):
        @pl.when(upper)
        def _():
            for side in ((0, 1) if dist > 0 else (0,)):
                if dist == 1:
                    got(kv_part(slot_of(0, side, 1), side, 1, KEY), kv_rs.at[1, side, 1])
                    kv_sib(1, side, 1, upper)
                v_across(side, dist)
            if dist == 0:
                for side in (0, 1):
                    kv_ring(1, side, 0, upper)

    def w_got(dist):
        for side in (0, 1):
            got(w_part(slot_of(0, side, dist), side, dist), w_rs.at[side, dist])
            if dist < 4:
                w_ring(side, dist)
            w_sib(side, dist)

    def own_row_got(dist):
        for side in (0, 1):
            got(kv_part(slot_of(y, side, dist), side, dist, ALL), kv_rs.at[0, side, dist])
            if dist < 4:
                kv_ring(0, side, dist)
            kv_sib(0, side, dist)

        @pl.when(lower)
        def _():
            for side in (0, 1):
                v_out(side, dist)

    def u_first_got():
        @pl.when(crossed)
        def _():
            got(ub.at[x, 0], u_rs.at[0, 0, 0])
            for side in (0, 1):
                u_ring(0, side, 0, crossed)

        got(ub.at[x, 1], u_rs.at[1, 0, 0])
        for side in (0, 1):
            u_ring(1, side, 0)

    def u_next_got(h):
        for side in (0, 1):
            u_got(h, side, 1)
            u_ring(h, side, 1)

    own_row_got(1)
    w_got(1)
    other_row_got(0)
    u_first_got()
    forward_own_row(1)
    own_row_got(2)
    w_got(2)
    other_row_got(1)
    forward_other_row(0)
    u_next_got(0)
    forward_own_row(2)
    own_row_got(3)
    w_got(3)
    other_row_got(2)
    u_next_got(1)
    forward_other_row(1)
    own_row_got(4)
    w_got(4)
    forward_own_row(3)
    other_row_got(3)
    forward_other_row(2)
    other_row_got(4)
    forward_other_row(3)
    forward_opposite()

    total = stat[1:2, :]
    inv = 1.0 / total
    stat[1:2, :] = inv
    attn_t = (ot[...] * inv).astype(BF).astype(F32)
    ot[...] = attn_t
    attn_rows = attn_t.T.astype(BF)
    for h in range(HEADS):
        attn[0, :, h * HEAD:(h + 1) * HEAD] = attn_rows[h * SLOTS:(h + 1) * SLOTS, :]
    send(None, lambda: copy(attn.at[0], attn.at[1], at_s.at[0], at_s.at[1], across))

    for h in (0, 1):
        for side in (0, 1):
            u_got(h, side, 2)
    for dist in range(0, 5):
        for side in ((0, 1) if dist > 0 else (0,)):
            w_sib_got(side, dist)

    def head_grads(h):
        doacc[h] = jnp.zeros((SLOTS, HEADS * HEAD), F32)

        def step(i, carry):
            doacc[h] += mm(ub[i, h], wb[pl.ds(4 * i, 4)].reshape(4 * 128, HEADS * HEAD))
            return carry

        lax.fori_loop(0, NX, step, 0)

    head_grads(1)
    dsend[...] = doacc[1].astype(BF)
    send(None, lambda: copy(dsend, drecv, do_s.at[0], do_s.at[1], across))
    head_grads(0)

    def pj_slot(j, core):
        return ((z + j) % NZ) * 2 + core

    def proj_swap(j):
        return copy(pj.at[pj_slot(j, 1 - k)], pjs.at[j], pjs_ss.at[j], pjs_rs.at[j], sibling)

    def proj_terms():
        got(attn.at[1], at_s.at[1])

        def step(i, carry):
            xx = (((z + NZ // 2) % NZ) // 2 + jnp.where(i < 2, i, 5 - i)) % NX
            block = ub[xx].reshape(PAIR, HEADS * HEAD).astype(F32)
            term = mm(block.T.astype(BF), attn[...].reshape(PAIR, HEADS * HEAD)).astype(BF)
            pj[pl.ds(4 * xx, 4)] = term.reshape(4, 128, HEADS * HEAD)
            for i in (0, 1):
                proj_swap((2 * xx + i + NZ - z) % NZ).start()
            return carry

        lax.fori_loop(0, NX, step, 0)
        for j in range(NZ):
            pending.append((None, lambda j=j: proj_swap(j)))

    def head_grads_done():
        got(drecv, do_s.at[1])
        for h in range(HEADS):
            cols = slice(h * HEAD, (h + 1) * HEAD)
            grads = (doacc[0, :, cols] + drecv[:, cols].astype(F32)).astype(BF)
            dor[h * SLOTS:(h + 1) * SLOTS, :] = grads
        stat[2:3, :] = jnp.sum(dor[...].astype(F32).T * ot[...], axis=0, keepdims=True)

    def backward_blocks(items):
        loaded = [load_pair(p) for p, _, _ in items]
        keys_t = jnp.concatenate([turned(keys) for keys, _ in loaded], axis=1)
        values = jnp.concatenate([values for _, values in loaded], axis=0)
        probs = jnp.concatenate([
            eb[p].astype(F32) * (jnp.exp2(mb[p, 0:1, :] - stat[0:1, :]) * stat[1:2, :])
            for p, _, _ in items], axis=0)
        grads = dor[...]
        value_grad = mm(probs.astype(BF), grads)
        pushes = lax.dot_general(values, grads, NT, preferred_element_type=F32)
        slopes = (probs * (pushes - stat[2:3, :])).astype(BF)
        key_grad = mm(slopes, qr[...])
        dqt[...] += mm(keys_t, slopes)
        for i, (_, q, j) in enumerate(items):
            rows = slice(i * PAIR, (i + 1) * PAIR)
            dkv[q, j, :, :, 0:HEAD] = (key_grad[rows] * SCALE).astype(BF).reshape(2, SLOTS, HEAD)
            dkv[q, j, :, :, HEAD:] = value_grad[rows].astype(BF).reshape(2, SLOTS, HEAD)

    def no_grads(j):
        dkv[0, j] = jnp.zeros((2, SLOTS, 2 * HEAD), BF)

    def j_of(side, dist):
        return dist if side == 0 else NZ - dist

    def swap_grads(dist, q):
        for side in sides_of(dist):
            j = j_of(side, dist)
            send(upper if q else None, lambda j=j: copy(
                dkv.at[q, j, 1 - k], sib.at[q, j], sib_ss.at[q, j], sib_rs.at[q, j], sibling))

    def backward_single(dist):
        there = chip_at(dist)
        needed = there <= z

        @pl.when(jnp.logical_and(upper, needed))
        def _():
            backward_blocks([(there, 1, dist), (y * NZ + there, 0, dist)])

        @pl.when(upper != needed)
        def _():
            backward_blocks([(there, jnp.where(upper, 1, 0), dist)])

        @pl.when(jnp.logical_not(needed))
        def _():
            no_grads(dist)

        @pl.when(upper)
        def _():
            swap_grads(dist, 1)

        swap_grads(dist, 0)

    def backward_other_row(dist):
        backward_blocks([(chip_at(dist), 1, dist), (chip_at(NZ - dist), 1, NZ - dist)])
        swap_grads(dist, 1)

    def backward_own_row(dist):
        behind, before = dist, NZ - dist
        near, far = z >= dist, z + dist >= NZ

        @pl.when(jnp.logical_and(near, far))
        def _():
            backward_blocks(
                [(y * NZ + chip_at(behind), 0, behind), (y * NZ + chip_at(before), 0, before)])

        @pl.when(near != far)
        def _():
            j = jnp.where(near, before, behind)
            backward_blocks([(y * NZ + chip_at(j), 0, j)])
            no_grads(NZ - j)

        @pl.when(jnp.logical_not(jnp.logical_or(near, far)))
        def _():
            no_grads(before)
            no_grads(behind)

        swap_grads(dist, 0)

    def add_into(ref, parts):
        value = ref[...].astype(F32)
        for part in parts:
            value = value + part[...].astype(F32)
        ref[...] = value.astype(BF)

    def kv_across(dist):
        for side in sides_of(dist):
            j = j_of(side, dist)
            got(sib.at[1, j], sib_rs.at[1, j])
            add_into(dkv.at[1, j, k], [sib.at[1, j]])
            send(upper, lambda j=j: copy(
                dkv.at[1, j, k], yvx.at[j], yv_ss.at[j], yv_rs.at[j], across))

    def kv_pass(dist):
        for side in sides_of(dist):
            j = j_of(side, dist)
            got(sib.at[0, j], sib_rs.at[0, j])
            parts = [sib.at[0, j]]
            for way in ((0, 1) if dist == 0 else (side,) if dist < 3 else ()):
                got(rrx.at[way, dist], rrx_rs.at[way, dist])
                parts.append(rrx.at[way, dist])

            @pl.when(lower)
            def _():
                got(yvx.at[j], yv_rs.at[j])
                add_into(dkv.at[0, j, k], parts + [yvx.at[j]])

            @pl.when(upper)
            def _():
                add_into(dkv.at[0, j, k], parts)

            if dist == 3:
                half = pl.ds(side * 96, 96)
                got(rrx.at[side, 3, half], rrx_rs.at[side, 3])
                add_into(dkv.at[0, j, k, half], [rrx.at[side, 3, half]])
        for side in ((0, 1) if dist > 0 else ()):
            def make(side=side):
                if dist == 4:
                    half = pl.ds(side * 96, 96)
                    src, dst = dkv.at[0, 4, k, half], rrx.at[side, 3, half]
                else:
                    src, dst = dkv.at[0, j_of(side, dist), k], rrx.at[side, dist - 1]
                return copy(src, dst, rrx_ss.at[side, dist - 1],
                            rrx_rs.at[side, dist - 1], ring[side])
            send(None, make)

    def proj_pass(dist):
        for side in sides_of(dist):
            j = j_of(side, dist)
            slot = pj_slot(j, k)
            got(pjs.at[j], pjs_rs.at[j])
            parts = [pjs.at[j]]
            if 0 < dist < 3:
                got(pjr.at[side, dist], pjr_rs.at[side, dist])
                parts.append(pjr.at[side, dist])
            elif dist == 0:
                for other in (0, 1):
                    got(pjr.at[other, 0], pjr_rs.at[other, 0])
                    parts.append(pjr.at[other, 0])
            add_into(pj.at[slot], parts)
            if dist == 3:
                half = pl.ds(side * 64, 64)
                got(pjr.at[side, 3, half], pjr_rs.at[side, 3])
                add_into(pj.at[slot, half], [pjr.at[side, 3, half]])
        if dist == 0:
            return
        for side in (0, 1):
            def make(side=side):
                if dist == 4:
                    half = pl.ds(side * 64, 64)
                    src, dst = pj.at[pj_slot(4, k), half], pjr.at[side, 3, half]
                else:
                    src, dst = pj.at[pj_slot(j_of(side, dist), k)], pjr.at[side, dist - 1]
                return copy(src, dst, pjr_ss.at[side, dist - 1],
                            pjr_rs.at[side, dist - 1], ring[side])
            send(None, make)

    proj_terms()
    proj_pass(4)
    head_grads_done()
    backward_single(4)
    for dist in (3, 2, 1):
        @pl.when(upper)
        def _():
            backward_other_row(dist)
            kv_across(dist + 1)

        kv_pass(dist + 1)
        backward_own_row(dist)
        proj_pass(dist)

    backward_single(0)

    @pl.when(upper)
    def _():
        kv_across(1)

    kv_pass(1)

    query_rows = (dqt[...] * SCALE).T.astype(BF)
    empty = jnp.zeros((TOKENS - SLOTS, HEAD), BF)
    for h in range(HEADS):
        part = jnp.concatenate([query_rows[h * SLOTS:(h + 1) * SLOTS, :], empty], axis=0)
        qo_ref[:, h * HEAD:(h + 1) * HEAD] = mm(pickt[...], part).astype(BF)

    @pl.when(upper)
    def _():
        kv_across(0)

    proj_pass(0)
    po_ref[...] = pj[pj_slot(0, k)]
    kv_pass(0)
    sums = jnp.concatenate(
        [dkv[0, 0, k], jnp.zeros((TOKENS - SLOTS, 2 * HEAD), BF)], axis=0)
    kvo_ref[...] = mm(pickt[...], sums).astype(BF)

    for cond, make in pending:
        if cond is None:
            make().wait_send()
        else:
            @pl.when(cond)
            def _():
                make().wait_send()


def shards(queries, keys_values, upstream, out_proj, keep_index):
    keep = keep_index.reshape(1, SLOTS)
    dma = pltpu.SemaphoreType.DMA
    width = HEADS * HEAD
    vmem = pltpu.VMEM
    scratch = [
        vmem((4 * NZ, ROWS, 2 * HEAD), BF),
        vmem((2 * NZ, 128, width), BF),
        vmem((NX, 2, SLOTS, width), BF),
        vmem((SLOTS, width), BF),
        vmem((2 * NZ, PAIR, QROWS), BF),
        vmem((2 * NZ, 8, QROWS), F32),
        vmem((QROWS, HEAD), BF),
        vmem((QROWS, HEAD), BF),
        vmem((HEAD, QROWS), F32),
        vmem((HEAD, QROWS), F32),
        vmem((8, QROWS), F32),
        vmem((TOKENS, TOKENS), BF),
        vmem((2, SLOTS, width), BF),
        vmem((2, SLOTS, width), F32),
        vmem((SLOTS, width), BF),
        vmem((SLOTS, width), BF),
        vmem((8, TOKENS), jnp.int32),
        vmem((2 * NZ, 128, width), BF),
        vmem((NZ, 128, width), BF),
        vmem((2, 4, 128, width), BF),
        vmem((2, NZ, 2, SLOTS, 2 * HEAD), BF),
        vmem((2, NZ, SLOTS, 2 * HEAD), BF),
        vmem((2, 4, SLOTS, 2 * HEAD), BF),
        vmem((NZ, SLOTS, 2 * HEAD), BF),
        dma((2, 2, 5)), dma((2, 2, 5)), dma((2, 2, 5)), dma((2, 2, 5)),
        dma((2, 5)), dma((2, 5)), dma((2, 5)), dma((2, 5)),
        dma((2, 5)), dma((2, 5)), dma((2, 5)), dma((2, 5)),
        dma((2, 2, 3)), dma((2, 2, 3)), dma((2,)), dma((2,)), dma((2,)),
        dma((NZ,)), dma((NZ,)), dma((2, 4)), dma((2, 4)),
        dma((2, NZ)), dma((2, NZ)), dma((2, 4)), dma((2, 4)),
        dma((NZ,)), dma((NZ,)),
    ]
    return pl.pallas_call(
        kernel,
        out_shape=(
            jax.ShapeDtypeStruct(queries.shape, BF),
            jax.ShapeDtypeStruct(keys_values.shape, BF),
            jax.ShapeDtypeStruct(out_proj.shape, BF),
        ),
        in_specs=[pl.BlockSpec(memory_space=pltpu.VMEM)] * 5,
        out_specs=[pl.BlockSpec(memory_space=pltpu.VMEM)] * 3,
        scratch_shapes=scratch,
        compiler_params=pltpu.CompilerParams(
            collective_id=0, has_side_effects=True, vmem_limit_bytes=56 * 1024 * 1024
        ),
    )(keep, queries, keys_values, upstream, out_proj)


def solution(mesh):
    in_specs = (P("ctx", "tp"), P("ctx", "tp"), P("ctx", "tp"), P("ctx", "tp"), P("ctx"))
    out_specs = (P("ctx", "tp"), P("ctx", "tp"), P("ctx", "tp"))
    return jax.shard_map(shards, mesh=mesh, in_specs=in_specs, out_specs=out_specs, check_vma=False)
```

time: 85.6 us -> 76.1 us (0.89); the launches traced: 83.9 us -> 76 us
  Pallas kernels: 79.9 us -> 72 us
    pallas_call x1, Pallas kernels: 79.9 us -> 72 us  [shards(): pl.pallas_call(kernel, out_shape=(jax.ShapeDtypeStruct(queries.shape, BF)...]
where the time goes in v3:
time: 76.1 us; the launch traced here: 76 us
  Pallas kernels  72 us (95%)
  local copies, waits for them, and re-layouts  3.31 us (4%)
    pallas_call x1, Pallas kernels, shards(): pl.pallas_call(kernel, out_shape=(jax.ShapeDtypeStruct(queries.shape, BF)...  72 us
    unnamed x7, local copies, waits for them, and re-layouts  3.31 us

profile of v3, /device:TPU:1, one launch (start us, length us, event | category | flops | bytes accessed | tf_op | source)
XLA Modules:
  0.0 76.0 jit_solution(2569990702241512167)
XLA Ops:
  0.6 72.0 %shard_map.76 = (bf16[256,512]{1,0:T(8,128)(2,1)}, bf16[256,256]{1,0:T(8,128)(2,1)}, bf16[128,512]{1,0:T(8,128)(2,1)}) custom-call(s32[1,192]{1,0:T(1,128)} %bitcast.1, bf16[256,512]{1,0:T(8,128)(2,1)} %q_ref.1, bf16[256,256]{1,0:T(8,128)(2,1)} %kv_ref.1, bf16[256,512]{1,0:T(8,128)(2,1)} %up_ref.1, bf16[128,512]{1,0:T(8,128)(2,1)} %w_ref.1), custom_call_target="tpu_custom_call" | custom-call | tf_op jit(solution)/shard_map/pallas_call | solution.py:695
  72.6 0.0 copy-start.1
  72.7 1.7 %copy.11 = bf16[256,512]{1,0:T(8,128)(2,1)} copy(bf16[256,512]{1,0:T(8,128)(2,1)} %get-tuple-element.6) | data formatting | bytes 524288
  74.4 0.0 copy-done.1
  74.4 0.0 copy-start
  74.4 0.7 copy.12
  75.0 0.3 copy-done
  75.3 0.7 copy.13
Async XLA Ops:
  72.6 1.7 %copy-start.1 = (bf16[256,256]{1,0:T(8,128)(2,1)S(1)}, bf16[256,256]{1,0:T(8,128)(2,1)}, u32[]{:S(2)}) copy-start(bf16[256,256]{1,0:T(8,128)(2,1)} %get-tuple-element.7) | copy-start | bytes 393220
  74.4 1.0 %copy-start = (bf16[128,512]{1,0:T(8,128)(2,1)S(1)}, bf16[128,512]{1,0:T(8,128)(2,1)}, u32[]{:S(2)}) copy-start(bf16[128,512]{1,0:T(8,128)(2,1)} %get-tuple-element.8) | copy-start | bytes 393220

commit v4 on v3

--- a/solution.py
+++ b/solution.py
@@ -370,21 +370,21 @@
     u_first_got()
     forward_own_row(1)
     own_row_got(2)
+    forward_other_row(0)
     w_got(2)
     other_row_got(1)
-    forward_other_row(0)
     u_next_got(0)
     forward_own_row(2)
     own_row_got(3)
+    forward_other_row(1)
     w_got(3)
     other_row_got(2)
     u_next_got(1)
-    forward_other_row(1)
     own_row_got(4)
+    forward_own_row(3)
+    forward_other_row(2)
     w_got(4)
-    forward_own_row(3)
     other_row_got(3)
-    forward_other_row(2)
     other_row_got(4)
     forward_other_row(3)
     forward_opposite()
@@ -426,9 +426,7 @@
     def proj_swap(j):
         return copy(pj.at[pj_slot(j, 1 - k)], pjs.at[j], pjs_ss.at[j], pjs_rs.at[j], sibling)
 
-    def proj_terms():
-        got(attn.at[1], at_s.at[1])
-
+    def proj_terms(first, last):
         def step(i, carry):
             xx = (((z + NZ // 2) % NZ) // 2 + jnp.where(i < 2, i, 5 - i)) % NX
             block = ub[xx].reshape(PAIR, HEADS * HEAD).astype(F32)
@@ -438,9 +436,7 @@
                 proj_swap((2 * xx + i + NZ - z) % NZ).start()
             return carry
 
-        lax.fori_loop(0, NX, step, 0)
-        for j in range(NZ):
-            pending.append((None, lambda j=j: proj_swap(j)))
+        lax.fori_loop(first, last, step, 0)
 
     def head_grads_done():
         got(drecv, do_s.at[1])
@@ -606,8 +602,12 @@
                             pjr_rs.at[side, dist - 1], ring[side])
             send(None, make)
 
-    proj_terms()
+    got(attn.at[1], at_s.at[1])
+    proj_terms(0, 2)
     proj_pass(4)
+    proj_terms(2, NX)
+    for j in range(NZ):
+        pending.append((None, lambda j=j: proj_swap(j)))
     head_grads_done()
     backward_single(4)
     for dist in (3, 2, 1):

time: 76.1 us -> 75.7 us (level)
  no operation moved by 1% of the time
where the time goes in v4:
time: 75.7 us; the launch traced here: 75.6 us
  Pallas kernels  71.6 us (95%)
  local copies, waits for them, and re-layouts  3.31 us (4%)
    pallas_call x1, Pallas kernels, shards(): pl.pallas_call(kernel, out_shape=(jax.ShapeDtypeStruct(queries.shape, BF)...  71.6 us
    unnamed x7, local copies, waits for them, and re-layouts  3.31 us

profile of v4, /device:TPU:1, one launch (start us, length us, event | category | flops | bytes accessed | tf_op | source)
XLA Modules:
  0.0 75.6 jit_solution(6164578026385531972)
XLA Ops:
  0.6 71.6 %shard_map.76 = (bf16[256,512]{1,0:T(8,128)(2,1)}, bf16[256,256]{1,0:T(8,128)(2,1)}, bf16[128,512]{1,0:T(8,128)(2,1)}) custom-call(s32[1,192]{1,0:T(1,128)} %bitcast.1, bf16[256,512]{1,0:T(8,128)(2,1)} %q_ref.1, bf16[256,256]{1,0:T(8,128)(2,1)} %kv_ref.1, bf16[256,512]{1,0:T(8,128)(2,1)} %up_ref.1, bf16[128,512]{1,0:T(8,128)(2,1)} %w_ref.1), custom_call_target="tpu_custom_call" | custom-call | tf_op jit(solution)/shard_map/pallas_call | solution.py:695
  72.3 0.0 copy-start.1
  72.3 1.7 %copy.11 = bf16[256,512]{1,0:T(8,128)(2,1)} copy(bf16[256,512]{1,0:T(8,128)(2,1)} %get-tuple-element.6) | data formatting | bytes 524288
  74.0 0.0 copy-done.1
  74.0 0.0 copy-start
  74.0 0.7 copy.12
  74.6 0.3 copy-done
  74.9 0.7 copy.13
Async XLA Ops:
  72.3 1.7 %copy-start.1 = (bf16[256,256]{1,0:T(8,128)(2,1)S(1)}, bf16[256,256]{1,0:T(8,128)(2,1)}, u32[]{:S(2)}) copy-start(bf16[256,256]{1,0:T(8,128)(2,1)} %get-tuple-element.7) | copy-start | bytes 393220
  74.0 1.0 %copy-start = (bf16[128,512]{1,0:T(8,128)(2,1)S(1)}, bf16[128,512]{1,0:T(8,128)(2,1)}, u32[]{:S(2)}) copy-start(bf16[128,512]{1,0:T(8,128)(2,1)} %get-tuple-element.8) | copy-start | bytes 393220

commit v5 on v4

--- a/solution.py
+++ b/solution.py
@@ -182,6 +182,7 @@
     def u_got(h, side, dist):
         got(u_part(h, side, dist, dist == 2), u_rs.at[h, side, dist])
 
+    kv_sib(0, 0, 0)
     for side in (0, 1):
         kv_ring(0, side, 0)
 
@@ -198,8 +199,6 @@
     def _():
         for side in (0, 1):
             u_ring(0, side, 0, aligned)
-
-    kv_sib(0, 0, 0)
 
     @pl.when(lower)
     def _():
@@ -263,12 +262,13 @@
         stat[0:1, :] = new
         stat[1:2, :] = stat[1:2, :] * shrink + sums[HEAD:HEAD + 1]
 
-    kv_sib_got(0, 0, 0)
-    forward_blocks([y * NZ + z], True)
-
     for side in (0, 1):
         w_ring(side, 0)
     w_sib(0, 0)
+
+    kv_sib_got(0, 0, 0)
+    forward_blocks([y * NZ + z], True)
+
 
     def sides_of(dist):
         return (0, 1) if 0 < dist < 4 else (0,)

time: 75.7 us -> 75.8 us (level)
  no operation moved by 1% of the time
where the time goes in v5:
time: 75.8 us; the launch traced here: 75.3 us
  Pallas kernels  71.4 us (94%)
  local copies, waits for them, and re-layouts  3.31 us (4%)
    pallas_call x1, Pallas kernels, shards(): pl.pallas_call(kernel, out_shape=(jax.ShapeDtypeStruct(queries.shape, BF)...  71.4 us
    unnamed x7, local copies, waits for them, and re-layouts  3.31 us

profile of v5, /device:TPU:1, one launch (start us, length us, event | category | flops | bytes accessed | tf_op | source)
XLA Modules:
  0.0 75.3 jit_solution(4447051490485747727)
XLA Ops:
  0.6 71.4 %shard_map.76 = (bf16[256,512]{1,0:T(8,128)(2,1)}, bf16[256,256]{1,0:T(8,128)(2,1)}, bf16[128,512]{1,0:T(8,128)(2,1)}) custom-call(s32[1,192]{1,0:T(1,128)} %bitcast.1, bf16[256,512]{1,0:T(8,128)(2,1)} %q_ref.1, bf16[256,256]{1,0:T(8,128)(2,1)} %kv_ref.1, bf16[256,512]{1,0:T(8,128)(2,1)} %up_ref.1, bf16[128,512]{1,0:T(8,128)(2,1)} %w_ref.1), custom_call_target="tpu_custom_call" | custom-call | tf_op jit(solution)/shard_map/pallas_call | solution.py:695
  72.0 0.0 copy-start.1
  72.0 1.7 %copy.11 = bf16[256,512]{1,0:T(8,128)(2,1)} copy(bf16[256,512]{1,0:T(8,128)(2,1)} %get-tuple-element.6) | data formatting | bytes 524288
  73.7 0.0 copy-done.1
  73.7 0.0 copy-start
  73.7 0.7 copy.12
  74.4 0.3 copy-done
  74.7 0.7 copy.13
Async XLA Ops:
  72.0 1.7 %copy-start.1 = (bf16[256,256]{1,0:T(8,128)(2,1)S(1)}, bf16[256,256]{1,0:T(8,128)(2,1)}, u32[]{:S(2)}) copy-start(bf16[256,256]{1,0:T(8,128)(2,1)} %get-tuple-element.7) | copy-start | bytes 393220
  73.7 1.0 %copy-start = (bf16[128,512]{1,0:T(8,128)(2,1)S(1)}, bf16[128,512]{1,0:T(8,128)(2,1)}, u32[]{:S(2)}) copy-start(bf16[128,512]{1,0:T(8,128)(2,1)} %get-tuple-element.8) | copy-start | bytes 393220
